TPU v7x, 32 devices: a whole 2x2x4 slice. The times are simulated.
32 devices in a mesh: dp: 2 (over x), hs: 4 (over z), blk: 4 (over y, core).
Axes of the slice: x: 2, y: 2, z: 4, core: 2. Of those that a mesh axis runs over, the one named last changes fastest.
Arguments:
- tokens: bfloat16 [6144, 2048], P(('dp', 'hs', 'blk')), may hold values from -6 to 6
- block_order: int32 [2, 16], P('dp'), may hold values from 0 to 15, each once within a row
- gain_attn: bfloat16 [2048], P(('dp', 'hs', 'blk')), may hold values from 0.5 to 1.5
- w_qkv: bfloat16 [2048, 6144], P(('dp', 'hs', 'blk')), may hold values from -0.125 to 0.125
- w_out: bfloat16 [2048, 2048], P(('dp', 'hs', 'blk')), may hold values from -4 to 4
- gain_mlp: bfloat16 [2048], P(('dp', 'hs', 'blk')), may hold values from 0.5 to 1.5
- w_gate_up: bfloat16 [2048, 16384], P(('dp', 'hs', 'blk')), may hold values from -0.125 to 0.125
- w_down: bfloat16 [2048, 8192], P(('dp', 'hs', 'blk')), may hold values from -0.0625 to 0.0625
- cotangent: bfloat16 [6144, 2048], P(('dp', 'hs', 'blk')), may hold values from -6 to 6
Outputs:
- layer_out: bfloat16 [6144, 2048], P(('dp', 'hs', 'blk'))
- grad_tokens: float32 [6144, 2048], P(('dp', 'hs', 'blk'))
- grad_gain_attn: float32 [2048], P(('dp', 'hs', 'blk'))
- grad_w_qkv: float32 [2048, 6144], P(('dp', 'hs', 'blk'))
- grad_w_out: float32 [2048, 2048], P(('dp', 'hs', 'blk'))
- grad_gain_mlp: float32 [2048], P(('dp', 'hs', 'blk'))
- grad_w_gate_up: float32 [2048, 16384], P(('dp', 'hs', 'blk'))
- grad_w_down: float32 [2048, 8192], P(('dp', 'hs', 'blk'))
Inputs may be any that keep to these rules, and one draw needn't show every extreme that they name: Each row of block_order names every block number of a sequence exactly once.
All inputs are finite; a program needn't handle non-finite values.
Results may differ from a plain program's by a relative error of at most 0.015.
Values may be sent and summed in bfloat16 or wider, within the bound.
A program may use at most 832 MiB of HBM per device.

v0:
```python
import jax
import jax.numpy as jnp
from jax import lax
from jax.sharding import PartitionSpec as P

HEADS = 32
HEAD_DIM = 64


THETA = 130000.0
EPS = 1e-05


def angles(positions, head_size):
    half = head_size // 2
    index = jnp.arange(half, dtype=jnp.float32)
    freq = jnp.power(jnp.float32(THETA), -2.0 * index / float(head_size))
    angle = positions.astype(jnp.float32)[:, None] * freq[None, :]
    return (jnp.cos(angle)[:, None, :], jnp.sin(angle)[:, None, :])


def rotate(values, positions, sign):
    half = values.shape[-1] // 2
    cosine, sine = angles(positions, values.shape[-1])
    sine = sine * sign
    first, second = (values[..., :half], values[..., half:])
    return jnp.concatenate(
        [first * cosine - second * sine, second * cosine + first * sine], axis=-1
    )


def rms_scale(values, gain):
    return values * lax.rsqrt(jnp.mean(values * values, axis=-1, keepdims=True) + EPS) * gain


def contract_rows(left, right):
    return lax.dot_general(
        left, right, (((0,), (0,)), ((), ())), preferred_element_type=jnp.float32
    )


def body(tokens, block_order, gain_attn, w_qkv, w_out, gain_mlp, w_gate_up, w_down, cotangent):
    n_heads_axis = lax.axis_size("hs")
    n_blk_axis = lax.axis_size("blk")
    tok_rows = tokens.shape[0]
    model_width = w_qkv.shape[1] // 3
    hidden_width = w_down.shape[1]
    heads_here = HEADS // n_heads_axis
    channels = model_width // n_heads_axis
    group_rows = n_heads_axis * tok_rows
    scale = HEAD_DIM ** (-0.5)
    head_pos = lax.axis_index("hs")
    blk_pos = lax.axis_index("blk")
    order = block_order[0]
    offsets = jnp.arange(tok_rows, dtype=jnp.int32)
    own_pos = order[head_pos * n_blk_axis + blk_pos] * tok_rows + offsets
    key_ids = order.reshape(n_heads_axis, n_blk_axis).T.reshape(-1)
    key_pos = (key_ids[:, None] * tok_rows + offsets[None, :]).reshape(-1)
    query_pos = lax.dynamic_slice_in_dim(key_pos, blk_pos * group_rows, group_rows)
    pos_blocks = key_pos.reshape(n_blk_axis, group_rows)
    gain_one, wqkv_full, wout_full = (
        lax.all_gather(gain_attn, ("dp", "hs", "blk"), axis=0, tiled=True),
        lax.all_gather(w_qkv, ("dp", "hs", "blk"), axis=0, tiled=True),
        lax.all_gather(w_out, ("dp", "hs", "blk"), axis=0, tiled=True),
    )
    gain_one_f = gain_one.astype(jnp.float32)
    x_float = tokens.astype(jnp.float32)
    xn1 = rms_scale(x_float, gain_one_f).astype(jnp.bfloat16)
    qkv = jnp.dot(xn1, wqkv_full, preferred_element_type=jnp.float32)
    query_rot = rotate(
        qkv[:, :model_width].reshape(tok_rows, HEADS, HEAD_DIM), own_pos, 1.0
    ).reshape(tok_rows, model_width)
    keys_rot = rotate(
        qkv[:, model_width : 2 * model_width].reshape(tok_rows, HEADS, HEAD_DIM), own_pos, 1.0
    ).reshape(tok_rows, model_width)
    packed = jnp.stack([query_rot, keys_rot, qkv[:, 2 * model_width :]], axis=1).astype(
        jnp.bfloat16
    )
    by_heads = lax.all_to_all(packed, "hs", split_axis=2, concat_axis=0, tiled=True)
    query = by_heads[:, 0].reshape(group_rows, heads_here, HEAD_DIM)
    kv_all = lax.all_gather(by_heads[:, 1:], "blk", axis=0, tiled=True)
    key_blocks = kv_all.reshape(n_blk_axis, group_rows, 2, heads_here, HEAD_DIM)

    def scores_of(kv_block, block_pos):
        raw = (
            jnp.einsum("qhd,khd->hqk", query, kv_block[:, 0], preferred_element_type=jnp.float32)
            * scale
        )
        allowed = (query_pos[:, None] >= block_pos[None, :])[None]
        return (jnp.where(allowed, raw, -1e30), allowed)

    def first_pass(carry, item):
        top, total = carry
        masked, allowed = scores_of(item[0], item[1])
        new_top = jnp.maximum(top, jnp.max(masked, axis=-1))
        expo = jnp.where(allowed, jnp.exp(masked - new_top[..., None]), 0.0)
        total = total * jnp.exp(top - new_top) + jnp.sum(expo, axis=-1)
        return ((new_top, total), None)

    start_top = jnp.full((heads_here, group_rows), -1e30, jnp.float32)
    start_total = jnp.zeros((heads_here, group_rows), jnp.float32)
    (top, total), _ = lax.scan(first_pass, (start_top, start_total), (key_blocks, pos_blocks))

    def probs_of(masked, allowed):
        return jnp.where(allowed, jnp.exp(masked - top[..., None]) / total[..., None], 0.0)

    def second_pass(acc, item):
        masked, allowed = scores_of(item[0], item[1])
        probs = probs_of(masked, allowed).astype(jnp.bfloat16)
        return (
            acc
            + jnp.einsum("hqk,khd->qhd", probs, item[0][:, 1], preferred_element_type=jnp.float32),
            None,
        )

    ctx_heads, _ = lax.scan(
        second_pass,
        jnp.zeros((group_rows, heads_here, HEAD_DIM), jnp.float32),
        (key_blocks, pos_blocks),
    )
    ctx_tok = lax.all_to_all(
        ctx_heads.reshape(group_rows, channels).astype(jnp.bfloat16),
        "hs",
        split_axis=0,
        concat_axis=1,
        tiled=True,
    )
    y_mid = x_float + jnp.dot(ctx_tok, wout_full, preferred_element_type=jnp.float32)
    gain_two, wgu_full, wdown_full = (
        lax.all_gather(gain_mlp, ("dp", "hs", "blk"), axis=0, tiled=True),
        lax.all_gather(w_gate_up, ("dp", "hs", "blk"), axis=0, tiled=True),
        lax.all_gather(w_down, ("dp", "hs", "blk"), axis=0, tiled=True),
    )
    gain_two_f = gain_two.astype(jnp.float32)
    xn2 = rms_scale(y_mid, gain_two_f).astype(jnp.bfloat16)
    gate_up = jnp.dot(xn2, wgu_full, preferred_element_type=jnp.float32)
    gate = gate_up[:, :hidden_width]
    up_part = gate_up[:, hidden_width:]
    sigma = jax.nn.sigmoid(gate)
    hidden = (gate * sigma * up_part).astype(jnp.bfloat16)
    layer_out = (
        y_mid + jnp.einsum("tf,df->td", hidden, wdown_full, preferred_element_type=jnp.float32)
    ).astype(jnp.bfloat16)
    unused_gain, wgu_back, wdown_back = (
        lax.all_gather(gain_mlp, ("dp", "hs", "blk"), axis=0, tiled=True),
        lax.all_gather(w_gate_up, ("dp", "hs", "blk"), axis=0, tiled=True),
        lax.all_gather(w_down, ("dp", "hs", "blk"), axis=0, tiled=True),
    )
    d_hidden = jnp.dot(cotangent, wdown_back, preferred_element_type=jnp.float32)
    d_gate = d_hidden * up_part * (sigma * (1.0 + gate * (1.0 - sigma)))
    d_up = d_hidden * gate * sigma
    d_gate_up = jnp.concatenate([d_gate, d_up], axis=1).astype(jnp.bfloat16)
    d_xn2 = jnp.einsum("te,de->td", d_gate_up, wgu_back, preferred_element_type=jnp.float32)
    unused_two, pull_two = jax.vjp(rms_scale, y_mid, gain_two_f)
    dy_norm, d_gain_two = pull_two(d_xn2)
    d_mid = cotangent.astype(jnp.float32) + dy_norm
    left_a = xn2
    left_b = cotangent
    mlp_rows = lax.psum_scatter(
        jnp.concatenate([contract_rows(left_a, d_gate_up), contract_rows(left_b, hidden)], axis=1),
        ("dp", "hs", "blk"),
        scatter_dimension=0,
        tiled=True,
    )
    gu_rows = mlp_rows[:, : 2 * hidden_width]
    down_rows = mlp_rows[:, 2 * hidden_width :]
    unused_gain_one, wqkv_back, wout_back = (
        lax.all_gather(gain_attn, ("dp", "hs", "blk"), axis=0, tiled=True),
        lax.all_gather(w_qkv, ("dp", "hs", "blk"), axis=0, tiled=True),
        lax.all_gather(w_out, ("dp", "hs", "blk"), axis=0, tiled=True),
    )
    d_mid_b = d_mid.astype(jnp.bfloat16)
    d_ctx = jnp.einsum("td,cd->tc", d_mid_b, wout_back, preferred_element_type=jnp.float32).astype(
        jnp.bfloat16
    )
    d_out_heads = lax.all_to_all(d_ctx, "hs", split_axis=1, concat_axis=0, tiled=True).reshape(
        group_rows, heads_here, HEAD_DIM
    )
    delta = jnp.sum(d_out_heads.astype(jnp.float32) * ctx_heads, axis=-1).T

    def back_pass(dq_acc, item):
        masked, allowed = scores_of(item[0], item[1])
        probs = probs_of(masked, allowed)
        d_probs = jnp.einsum(
            "qhd,khd->hqk", d_out_heads, item[0][:, 1], preferred_element_type=jnp.float32
        )
        d_scores = (probs * (d_probs - delta[..., None])).astype(jnp.bfloat16)
        dq_acc = dq_acc + jnp.einsum(
            "hqk,khd->qhd", d_scores, item[0][:, 0], preferred_element_type=jnp.float32
        )
        d_keys = (
            jnp.einsum("hqk,qhd->khd", d_scores, query, preferred_element_type=jnp.float32) * scale
        )
        d_vals = jnp.einsum(
            "hqk,qhd->khd",
            probs.astype(jnp.bfloat16),
            d_out_heads,
            preferred_element_type=jnp.float32,
        )
        return (dq_acc, jnp.stack([d_keys, d_vals], axis=1).reshape(group_rows, 2, channels))

    dq_acc, dkv_blocks = lax.scan(
        back_pass,
        jnp.zeros((group_rows, heads_here, HEAD_DIM), jnp.float32),
        (key_blocks, pos_blocks),
    )
    dkv_own = lax.psum_scatter(
        dkv_blocks.reshape(n_blk_axis * group_rows, 2, channels).astype(jnp.bfloat16),
        "blk",
        scatter_dimension=0,
        tiled=True,
    ).astype(jnp.float32)
    dq_rows = (dq_acc * scale).reshape(group_rows, 1, channels)
    d_packed = jnp.concatenate([dq_rows, dkv_own], axis=1).astype(jnp.bfloat16)
    d_tok = lax.all_to_all(d_packed, "hs", split_axis=0, concat_axis=2, tiled=True)
    dq_pre = rotate(
        d_tok[:, 0].astype(jnp.float32).reshape(tok_rows, HEADS, HEAD_DIM), own_pos, -1.0
    ).reshape(tok_rows, model_width)
    dk_pre = rotate(
        d_tok[:, 1].astype(jnp.float32).reshape(tok_rows, HEADS, HEAD_DIM), own_pos, -1.0
    ).reshape(tok_rows, model_width)
    d_qkv = jnp.concatenate([dq_pre, dk_pre, d_tok[:, 2].astype(jnp.float32)], axis=1).astype(
        jnp.bfloat16
    )
    d_xn1 = jnp.einsum("te,de->td", d_qkv, wqkv_back, preferred_element_type=jnp.float32)
    unused_one, pull_one = jax.vjp(rms_scale, x_float, gain_one_f)
    dx_norm, d_gain_one = pull_one(d_xn1)
    grad_tokens = d_mid + dx_norm
    left_a = xn1
    left_b = ctx_tok
    attn_rows = lax.psum_scatter(
        jnp.concatenate([contract_rows(left_a, d_qkv), contract_rows(left_b, d_mid_b)], axis=1),
        ("dp", "hs", "blk"),
        scatter_dimension=0,
        tiled=True,
    )
    qkv_rows = attn_rows[:, : 3 * model_width]
    out_rows = attn_rows[:, 3 * model_width :]
    grad_gain_one, grad_gain_two = (
        lax.psum_scatter(d_gain_one, ("dp", "hs", "blk"), scatter_dimension=0, tiled=True),
        lax.psum_scatter(d_gain_two, ("dp", "hs", "blk"), scatter_dimension=0, tiled=True),
    )
    return (
        layer_out,
        grad_tokens,
        grad_gain_one,
        qkv_rows,
        out_rows,
        grad_gain_two,
        gu_rows,
        down_rows,
    )


def solution(mesh):
    in_specs = (
        P(("dp", "hs", "blk"), None),
        P("dp", None),
        P(("dp", "hs", "blk")),
        P(("dp", "hs", "blk"), None),
        P(("dp", "hs", "blk"), None),
        P(("dp", "hs", "blk")),
        P(("dp", "hs", "blk"), None),
        P(("dp", "hs", "blk"), None),
        P(("dp", "hs", "blk"), None),
    )
    out_specs = (
        P(("dp", "hs", "blk"), None),
        P(("dp", "hs", "blk"), None),
        P(("dp", "hs", "blk")),
        P(("dp", "hs", "blk"), None),
        P(("dp", "hs", "blk"), None),
        P(("dp", "hs", "blk")),
        P(("dp", "hs", "blk"), None),
        P(("dp", "hs", "blk"), None),
    )
    return jax.shard_map(body, mesh=mesh, in_specs=in_specs, out_specs=out_specs, check_vma=False)
```

profile of v0, /device:TPU:13, one launch (start us, length us, event | category | flops | bytes accessed | tf_op | source)
XLA Modules:
  0.0 3817.2 jit_solution(17762898493595597932)
XLA Ops:
  9.7 41.1 %all-reduce.5 = (bf16[2048]{0:T(1024)(128)(2,1)S(1)}, bf16[2048]{0:T(1024)(128)(2,1)}) all-reduce(bf16[2048]{0:T(1024)(128)(2,1)S(1)} %dynamic-update-slice, bf16[2048]{0:T(1024)(128)(2,1)S(1)} %dynamic-update-slice.1), channel_id=1, replica_groups=mesh['dp'=2,'hs'=4,'blk'=4] {'dp','hs','blk'}, use_global_device_ids=true, to_apply=%add | all-reduce | flops 4096 | bytes 16384
  55.5 110.9 %all-gather.6.cloned.1.call-done = bf16[2048,6144]{1,0:T(8,128)(2,1)} async-done(((bf16[64,6144]{1,0:T(8,128)(2,1)}), bf16[2048,6144]{1,0:T(8,128)(2,1)}) %all-gather.6.cloned.1.call-update) | async-done | bytes 25165840 | tf_op jit(solution)/shard_map/all_gather | solution.py:63
  166.5 11.1 fusion.42
  195.9 98.9 %all_to_all.68 = bf16[192,3,2048]{0,1,2:T(4,128)(2,1)} all-to-all(bf16[192,3,2048]{0,1,2:T(4,128)(2,1)} %copy.115), channel_id=1, replica_groups=mesh['dp'=2,'hs'=4,'blk'=4] {'hs'}, dimensions={2} | all-to-all | bytes 4718592 | tf_op jit(solution)/shard_map/all_to_all | solution.py:79
  305.5 42.3 %all-gather.8.cloned.1.call-done = bf16[3072,2,512]{2,0,1:T(8,128)(2,1)} async-done(((bf16[768,2,512]{2,0,1:T(8,128)(2,1)}), bf16[3072,2,512]{2,0,1:T(8,128)(2,1)}) %all-gather.8.cloned.1.call-update) | async-done | bytes 6291472 | tf_op jit(solution)/shard_map/all_gather | solution.py:81
  347.8 16.3 reshape.317
  364.1 13.1 copy.123
  377.2 90.4 %while.37 = (s32[]{:T(128)}, f32[8,768]{1,0:T(8,128)S(1)}, f32[8,768]{1,0:T(8,128)S(1)}, s32[768]{0:T(1024)S(1)}, s32[4,768]{1,0:T(4,128)S(1)}, /*index=5*/bf16[...) while((s32[]{:T(128)}, f32[8,768]{1,0:T(8,128)S(1)}, ...), condition=%wide.region_4.5_spmd.clone, body=%wide.region_1.4_spmd.clone.sunk | while | flops 642349056 | bytes 44568692 | solution.py:102
  433.5 11.7 select_reduce_fusion.2
  467.6 47.8 %while.38 = (s32[]{:T(128)}, f32[768,8,64]{0,2,1:T(8,128)}, bf16[4,768,2,8,64]{1,4,3,2,0:T(8,128)(2,1)}, s32[768]{0:T(1024)S(1)}, s32[4,768]{1,0:T(4,128)S(1)}, ...) while((s32[]{:T(128)}, f32[768,8,64]{0,2,1:T(8,128)}, ...), condition=%wide.region_6.7_spmd.clone, body=%wide.region_5.6_spmd.clone.sunk | while | flops 1237647360 | bytes 9891967 | solution.py:116
  523.9 37.2 all-to-all-done.1
  567.0 233.3 %all-gather.12.cloned.1.call-done = bf16[2048,16384]{1,0:T(8,128)(2,1)} async-done(((bf16[64,16384]{1,0:T(8,128)(2,1)}), bf16[2048,16384]{1,0:T(8,128)(2,1)}) %all-gather.12.cloned.1.call-update) | async-done | bytes 67108880 | tf_op jit(solution)/shard_map/all_gather | solution.py:131
  800.3 29.6 fusion.50
  829.9 166.1 %all-gather.14.cloned.1.call-done = bf16[2048,8192]{1,0:T(8,128)(2,1)} async-done(((bf16[64,8192]{1,0:T(8,128)(2,1)}), bf16[2048,8192]{1,0:T(8,128)(2,1)}) %all-gather.14.cloned.1.call-update) | async-done | bytes 33554448 | tf_op jit(solution)/shard_map/all_gather | solution.py:132
  996.1 26.9 multiply_convert_fusion.1
  1023.0 31.4 multiply_reduce_fusion
  1069.7 17.0 all-to-all-done.2
  1088.9 189.6 %while.39 = (s32[]{:T(128)}, f32[768,8,64]{0,2,1:T(8,128)}, bf16[4,768,2,512]{3,1,0,2:T(8,128)(2,1)}, bf16[4,768,2,8,64]{1,4,3,2,0:T(8,128)(2,1)}, s32[768]{0:T(...) while((s32[]{:T(128)}, f32[768,8,64]{0,2,1:T(8,128)}, ...), condition=%wide.region_11.12_spmd.clone, body=%wide.region_10.11_spmd.clone.sunk | while | flops 3065315328 | bytes 153047280 | solution.py:202
  1091.8 10.9 fusion.102
  1186.3 10.9 fusion.102
  1280.4 57.1 %reduce-scatter.4.cloned.1.call-done = bf16[768,2,512]{2,0,1:T(8,128)(2,1)} async-done(((bf16[3072,2,512]{2,0,1:T(8,128)(2,1)}), bf16[768,2,512]{2,0,1:T(8,128)(2,1)}) %reduce-scatter.4.cloned.1.call-update) | async-done | bytes 1572880 | tf_op jit(solution)/shard_map/reduce_scatter | solution.py:207
  1355.8 58.9 %all-to-all-done.3 = bf16[768,3,512]{2,1,0:T(4,128)(2,1)} async-done(((bf16[768,3,512]{2,1,0:T(4,128)(2,1)}), bf16[768,3,512]{2,1,0:T(4,128)(2,1)}, u32[]{:S(2)}, u32[]{:S(2)}) %all-to-all-start.3) | async-done | bytes 2359328 | tf_op jit(solution)/shard_map/all_to_all | solution.py:215
  1431.5 20.8 fusion.35
  1452.3 43.4 %pad_maximum_fusion.2 = f32[2048,8192]{1,0:T(8,128)} fusion(f32[2048,2048]{1,0:T(8,128)} %fusion.38, f32[2048,6144]{1,0:T(8,128)} %fusion.35), kind=kLoop, calls=%fused_computation.47 | loop fusion | flops 16777216 | bytes 134217728 | tf_op jit(solution)/shard_map/concatenate | solution.py:232
  1496.9 26.6 convolution_bitcast_fusion
  1523.5 47.6 %fusion.24 = f32[2048,16384]{1,0:T(8,128)} fusion(bf16[192,8192]{1,0:T(8,128)(2,1)} %get-tuple-element.413, bf16[192,8192]{1,0:T(8,128)(2,1)} %get-tuple-element.412, f32[192,2048]{1,0:T(8,128)S(1)} %copy-done.4, f32[2048]{0:T(1024)S(1)} %copy-done.20, f32[192]{0:T(256)S(1)} %copy-done.22), kind=kOutput, calls=%fused_computation.54 | convolution fusion | flops 12898664448 | bytes 142091008 | tf_op jit(solution)/shard_map/dot_general | solution.py:37
  1571.1 132.2 %pad_maximum_fusion.1 = f32[2048,24576]{1,0:T(8,128)} fusion(f32[2048,8192]{1,0:T(8,128)} %convolution_bitcast_fusion, f32[2048,16384]{1,0:T(8,128)} %fusion.24), kind=kLoop, calls=%fused_computation.46 | loop fusion | flops 50331648 | bytes 402653184 | tf_op jit(solution)/shard_map/concatenate | solution.py:160
  1704.7 18.0 fusion.26
  1722.7 14.9 fusion.30
  1737.7 48.0 %all-reduce.4 = (f32[2048]{0:T(1024)S(1)}, f32[2048]{0:T(1024)S(1)}) all-reduce(f32[2048]{0:T(1024)S(1)} %get-tuple-element.352, f32[2048]{0:T(1024)S(1)} %copy-done.34), channel_id=3, replica_groups=mesh['dp'=2,'hs'=4,'blk'=4] {'dp','hs','blk'}, use_global_device_ids=true, to_apply=%region_15.16.clone | all-reduce | flops 4096 | bytes 32768
  1789.8 411.7 %reduce-scatter.6.cloned.1.call-done = f32[64,8192]{1,0:T(8,128)} async-done(((f32[2048,8192]{1,0:T(8,128)}), f32[64,8192]{1,0:T(8,128)}) %reduce-scatter.6.cloned.1.call-update) | async-done | bytes 2097168 | tf_op jit(solution)/shard_map/reduce_scatter | solution.py:231
  2206.0 1596.5 %reduce-scatter.8.cloned.1.call-done = f32[64,24576]{1,0:T(8,128)} async-done(((f32[2048,24576]{1,0:T(8,128)}), f32[64,24576]{1,0:T(8,128)}) %reduce-scatter.8.cloned.1.call-update) | async-done | bytes 6291472 | tf_op jit(solution)/shard_map/reduce_scatter | solution.py:159
  (280 shorter events, 416.4 us)
Async XLA Ops:
  7.2 159.3 %all-gather.6.cloned.1.call-start = ((), (), s32[]{:S(2)}) async-start(), calls=%async_computation.7 | async-start | bytes 25952256 | tf_op jit(solution)/shard_map/all_gather | solution.py:63
  7.9 339.9 %all-gather.8.cloned.1.call-start = ((), (), s32[]{:S(2)}) async-start(), calls=%async_computation.8 | async-start | bytes 7864320 | tf_op jit(solution)/shard_map/all_gather | solution.py:81
  50.8 126.8 %copy-start.23 = (f32[2048]{0:T(1024)}, f32[2048]{0:T(1024)S(1)}, u32[]{:S(2)}) copy-start(f32[2048]{0:T(1024)S(1)} %convert_element_type.89) | copy-start | bytes 24580
  54.7 122.9 %copy-start.29 = (f32[192]{0:T(256)}, f32[192]{0:T(256)S(1)}, u32[]{:S(2)}) copy-start(f32[192]{0:T(256)S(1)} %fusion.44) | copy-start | bytes 2308
  55.5 129.6 %copy-start.26 = (f32[192,32]{0,1:T(8,128)}, f32[192,32]{0,1:T(8,128)S(1)}, u32[]{:S(2)}) copy-start(f32[192,32]{0,1:T(8,128)S(1)} %get-tuple-element.434) | copy-start | bytes 73732
  301.6 259.7 %all-gather.10.cloned.1.call-start = ((), (), s32[]{:S(2)}) async-start(), calls=%async_computation.9 | async-start | bytes 8650752 | tf_op jit(solution)/shard_map/all_gather | solution.py:64
  302.3 498.0 %all-gather.12.cloned.1.call-start = ((), (), s32[]{:S(2)}) async-start(), calls=%async_computation.10 | async-start | bytes 69206016 | tf_op jit(solution)/shard_map/all_gather | solution.py:131
  302.9 693.1 %all-gather.14.cloned.1.call-start = ((), (), s32[]{:S(2)}) async-start(), calls=%async_computation.11 | async-start | bytes 34603008 | tf_op jit(solution)/shard_map/all_gather | solution.py:132
  516.9 44.4 %copy-start.9 = (bf16[192,2048]{1,0:T(8,128)(2,1)S(1)}, bf16[192,2048]{1,0:T(8,128)(2,1)}, u32[]{:S(2)}) copy-start(bf16[192,2048]{1,0:T(8,128)(2,1)} %param.15) | copy-start | bytes 2359300
  519.2 41.9 %all-to-all-start.1 = ((bf16[4,192,512]{2,1,0:T(8,128)(2,1)}), bf16[4,192,512]{2,1,0:T(8,128)(2,1)S(1)}, u32[]{:S(2)}, u32[]{:S(2)}) async-start(bf16[4,192,512]{2,1,0:T(8,128)(2,1)} %copy.124), calls=%async_computation.1 | async-start | bytes 1572864 | tf_op jit(solution)/shard_map/all_to_all | solution.py:121
  523.9 530.5 %copy-start.19 = (f32[2048]{0:T(1024)}, f32[2048]{0:T(1024)S(1)}, u32[]{:S(2)}) copy-start(f32[2048]{0:T(1024)S(1)} %convert_element_type.94) | copy-start | bytes 24580
  566.9 487.4 %copy-start.3 = (f32[192,2048]{1,0:T(8,128)}, f32[192,2048]{1,0:T(8,128)S(1)}, u32[]{:S(2)}) copy-start(f32[192,2048]{1,0:T(8,128)S(1)} %get-tuple-element.436) | copy-start | bytes 4718596
  567.0 487.4 %copy-start.21 = (f32[192]{0:T(256)}, f32[192]{0:T(256)S(1)}, u32[]{:S(2)}) copy-start(f32[192]{0:T(256)S(1)} %fusion.45) | copy-start | bytes 2308
  800.3 195.7 %copy-start.13 = (bf16[192,2048]{1,0:T(8,128)(2,1)S(1)}, bf16[192,2048]{1,0:T(8,128)(2,1)}, u32[]{:S(2)}) copy-start(bf16[192,2048]{1,0:T(8,128)(2,1)} %param.23) | copy-start | bytes 2359300
  1063.2 25.6 copy-start.12
  1064.1 22.6 all-to-all-start.2
  1069.7 267.8 %reduce-scatter.4.cloned.1.call-start = ((), (), s32[]{:S(2)}) async-start(), calls=%async_computation.12 | async-start | bytes 7864320 | tf_op jit(solution)/shard_map/reduce_scatter | solution.py:207
  1170.0 7.1 copy-start
  1342.8 71.9 %all-to-all-start.3 = ((bf16[768,3,512]{2,1,0:T(4,128)(2,1)}), bf16[768,3,512]{2,1,0:T(4,128)(2,1)}, u32[]{:S(2)}, u32[]{:S(2)}) async-start(bf16[768,3,512]{2,1,0:T(4,128)(2,1)} %copy.131), calls=%async_computation.4 | async-start | bytes 6291456 | tf_op jit(solution)/shard_map/all_to_all | solution.py:215
  1347.7 853.8 %reduce-scatter.6.cloned.1.call-start = ((), (), s32[]{:S(2)}) async-start(), calls=%async_computation.13 | async-start | bytes 69206016 | tf_op jit(solution)/shard_map/reduce_scatter | solution.py:231
  1419.6 11.9 copy-start.17
  1495.8 2306.8 %reduce-scatter.8.cloned.1.call-start = ((), (), s32[]{:S(2)}) async-start(), calls=%async_computation.14 | async-start | bytes 207618048 | tf_op jit(solution)/shard_map/reduce_scatter | solution.py:159
  1496.9 26.6 copy-start.4
  1496.9 26.6 copy-start.20
  1496.9 26.6 copy-start.22
  1704.7 18.0 copy-start.11
  1704.7 18.0 copy-start.18
  1704.7 18.0 copy-start.25
  1704.7 18.0 copy-start.31
  1722.7 14.9 copy-start.34
  1722.7 64.1 %copy-start.33 = (f32[192]{0:T(256)S(1)}, f32[192]{0:T(256)}, u32[]{:S(2)}) copy-start(f32[192]{0:T(256)} %copy-done.32) | copy-start | bytes 2308
  1722.7 64.1 %copy-start.8 = (f32[192,2048]{1,0:T(8,128)S(1)}, f32[192,2048]{1,0:T(8,128)}, u32[]{:S(2)}) copy-start(f32[192,2048]{1,0:T(8,128)} %copy-done.6) | copy-start | bytes 4718596
  (25 other events, 85.8 us)
Sparse Core Ops, SparseCore 0:
  10.9 155.5 all-gather.5
  301.7 46.0 all-gather.7
  350.7 78.5 all-gather.9
  432.0 368.2 all-gather.11
  803.0 192.9 all-gather.13
  1278.7 58.7 reduce-scatter.3
  1495.9 705.5 reduce-scatter.5
  2209.1 1593.4 reduce-scatter.7
where the time goes:
time: 3830 us; the launch traced here: 3820 us
  waiting for transfers between devices  2730 us (71%)
  matrix products  494 us (13%)
  other arithmetic  250 us (7%)
  blocking collectives  188 us (5%)
  local copies, waits for them, and re-layouts  120 us (3%)
    reduce_scatter x1, waiting for transfers between devices, body(): lax.psum_scatter(jnp.concatenate([contract_rows(left_a, d_gate_up), contr...  1600 us
    reduce_scatter x1, waiting for transfers between devices, body(): lax.psum_scatter(jnp.concatenate([contract_rows(left_a, d_qkv), contract_...  412 us
    all_gather x1, waiting for transfers between devices, body(): lax.all_gather(w_gate_up, ('dp', 'hs', 'blk'), axis=0, tiled=True)  233 us
    all_gather x1, waiting for transfers between devices, body(): lax.all_gather(w_down, ('dp', 'hs', 'blk'), axis=0, tiled=True)  166 us
    concatenate x1, other arithmetic, body(): jnp.concatenate([contract_rows(left_a, d_gate_up), contract_rows(left_b,...  132 us
    all_gather x1, waiting for transfers between devices, body(): lax.all_gather(w_qkv, ('dp', 'hs', 'blk'), axis=0, tiled=True)  111 us
    dot_general x4, matrix products, contract_rows(): lax.dot_general(left, right, (((0,), (0,)), ((), ())), preferred_element_...  103 us
    all_to_all x1, blocking collectives, body(): lax.all_to_all(packed, 'hs', split_axis=2, concat_axis=0, tiled=True)  98.9 us
  transfers between devices with their start and end apart: 11, of which 10 were waited for; matrix products, arithmetic and copies ran while one was open for 12% of the time, Pallas kernels for 0%

commit v1 on v0

v1 whole, which is shorter than its diff:
```python
import functools

import jax
import jax.numpy as jnp
import numpy as np
from jax import lax
from jax.experimental import pallas as pl
from jax.experimental.pallas import tpu as pltpu
from jax.sharding import PartitionSpec as P

HEADS = 32
HEAD_DIM = 64
THETA = 130000.0
EPS = 1e-05
TP = ("hs", "blk")
ALL = ("dp", "hs", "blk")
VMEM_LIMIT = 56 * 1024 * 1024
EXP2_SCALE = HEAD_DIM**-0.5 * 1.4426950408889634

F32 = jnp.float32
BF16 = jnp.bfloat16


def dot_nn(a, b):
    return lax.dot_general(a, b, (((1,), (0,)), ((), ())), preferred_element_type=F32)


def dot_nt(a, b):
    return lax.dot_general(a, b, (((1,), (1,)), ((), ())), preferred_element_type=F32)


def dot_tn(a, b):
    return lax.dot_general(a, b, (((0,), (0,)), ((), ())), preferred_element_type=F32)


def rms_scale(values, gain):
    return values * lax.rsqrt(jnp.mean(values * values, axis=-1, keepdims=True) + EPS) * gain


def rope_tables(blocks, block):
    half = HEAD_DIM // 2
    lane = np.arange(2 * HEAD_DIM)
    index = jnp.asarray(lane % half, F32)
    sign = jnp.asarray(np.where(lane % HEAD_DIM < half, -1.0, 1.0), F32)
    freq = jnp.power(F32(THETA), -2.0 * index / float(HEAD_DIM))[None, :]
    base = (jnp.arange(blocks, dtype=jnp.int32) * block).astype(F32)[:, None] * freq
    step = jnp.arange(block, dtype=jnp.int32).astype(F32)[:, None] * freq
    cos, sin = jnp.cos(step), jnp.sin(step)
    return (
        jnp.stack([jnp.cos(base), jnp.sin(base)]),
        jnp.stack([cos, sin, cos * sign, sin * sign]),
    )


def rope_of_block(base_ref, step_ref, b):
    cos, sin = base_ref[0, pl.ds(b, 1), :], base_ref[1, pl.ds(b, 1), :]
    return (
        cos * step_ref[0] - sin * step_ref[1],
        sin * step_ref[2] + cos * step_ref[3],
    )


def swap_halves(x):
    half = HEAD_DIM // 2
    width = x.shape[1]
    lane = lax.broadcasted_iota(jnp.int32, x.shape, 1)
    return jnp.where(
        lax.rem(lane, HEAD_DIM) < half,
        pltpu.roll(x, width - half, 1),
        pltpu.roll(x, half, 1),
    )


MESH = pl.DeviceIdType.MESH
CHUNKS = 2


def position():
    z, b = lax.axis_index("hs"), lax.axis_index("blk")
    return z, b // 2, b % 2


def remote(src, dst, send, recv, **where):
    return pltpu.make_async_remote_copy(
        src_ref=src, dst_ref=dst, send_sem=send, recv_sem=recv, device_id=where, device_id_type=MESH
    )


def signal(sem, **where):
    pl.semaphore_signal(sem, inc=1, device_id=where, device_id_type=MESH)


def greet_neighbours(nz):
    z, y, c = position()
    barrier = pltpu.get_barrier_semaphore()
    signal(barrier, blk=y * 2 + 1 - c)
    signal(barrier, blk=(1 - y) * 2 + c)

    @pl.when(z > 0)
    def _():
        signal(barrier, hs=z - 1)

    @pl.when(z < nz - 1)
    def _():
        signal(barrier, hs=z + 1)

    count = 2 + jnp.where(z > 0, 1, 0) + jnp.where(z < nz - 1, 1, 0)
    pl.semaphore_wait(barrier, count)


def greet_all(nz, n_dp):
    z, y, c = position()
    peers = nz * 4
    me = z * 4 + y * 2 + c
    d = lax.axis_index("dp")
    barrier = pltpu.get_barrier_semaphore()

    @pl.loop(1, peers)
    def _(r):
        t = (me + r) % peers
        signal(barrier, hs=t // 4, blk=t % 4)

    @pl.loop(1, n_dp)
    def _(r):
        signal(barrier, dp=(d + r) % n_dp)

    pl.semaphore_wait(barrier, peers - 1 + n_dp - 1)


def by_distance(z, n, nz):
    near = jnp.minimum(z, nz - 1 - z)
    step = (n + 1) // 2
    both = jnp.where(n % 2 == 1, z - step, z + step)
    one = jnp.where(z < nz - 1 - z, n, nz - 1 - n)
    return jnp.where(n <= 2 * near, both, one)


def gather_sems(nz, chunks=CHUNKS):
    one, two = (nz, chunks), (nz, 2, chunks)
    return [pltpu.SemaphoreType.DMA(s) for s in (one, one, two, one, one, one, two)]


class Gather:
    def __init__(self, buf, sems, nz, lead=(), chunks=CHUNKS):
        self.buf, self.nz, self.lead, self.chunks = buf, nz, lead, chunks
        self.z, self.y, self.c = position()
        self.r_z, self.r_y, self.r_c, self.s_r, self.s_l, self.s_y, self.s_c = sems
        self.rows = buf.shape[-2] // chunks

    def part(self, zs, y, c, q):
        rows = pl.ds(pl.multiple_of(q * self.rows, self.rows), self.rows)
        return self.buf.at[(*self.lead, zs, y, c, rows, slice(None))]

    def right(self, zs, q):
        p = self.part(zs, self.y, self.c, q)
        return remote(p, p, self.s_r.at[zs, q], self.r_z.at[zs, q], hs=self.z + 1)

    def left(self, zs, q):
        p = self.part(zs, self.y, self.c, q)
        return remote(p, p, self.s_l.at[zs, q], self.r_z.at[zs, q], hs=self.z - 1)

    def across(self, zs, q):
        p = self.part(zs, self.y, self.c, q)
        return remote(
            p, p, self.s_y.at[zs, q], self.r_y.at[zs, q], blk=(1 - self.y) * 2 + self.c
        )

    def sibling(self, zs, y, q):
        p = self.part(zs, y, self.c, q)
        return remote(
            p, p, self.s_c.at[zs, y, q], self.r_c.at[zs, y, q], blk=self.y * 2 + 1 - self.c
        )

    def goes_right(self, zs):
        return jnp.logical_and(zs <= self.z, self.z < self.nz - 1)

    def goes_left(self, zs):
        return jnp.logical_and(zs >= self.z, self.z > 0)

    def row_part(self, n, q):
        zs = by_distance(self.z, n, self.nz)

        @pl.when(n > 0)
        def _():
            p = self.part(zs, self.y, self.c, q)
            remote(
                p, p, self.s_y.at[zs, q], self.r_z.at[zs, q], blk=self.y * 2 + 1 - self.c
            ).wait_recv()

        @pl.when(self.goes_right(zs))
        def _():
            self.right(zs, q).start()

        @pl.when(self.goes_left(zs))
        def _():
            self.left(zs, q).start()

        self.across(zs, q).start()
        self.sibling(zs, self.y, q).start()

    def cross_part(self, n, q):
        zs = by_distance(self.z, n, self.nz)
        p = self.part(zs, 1 - self.y, self.c, q)
        remote(
            p, p, self.s_y.at[zs, q], self.r_y.at[zs, q], blk=(1 - self.y) * 2 + self.c
        ).wait_recv()
        self.sibling(zs, 1 - self.y, q).start()

    def row_step(self, n):
        for q in range(self.chunks):
            self.row_part(n, q)

    def cross_step(self, n):
        for q in range(self.chunks):
            self.cross_part(n, q)

    def chunk_step(self, e):
        @pl.when(e < self.nz * self.chunks)
        def _():
            self.row_part(e // self.chunks, e % self.chunks)

        self.cross_part((e - self.chunks) // self.chunks, e % self.chunks)

    def ready(self, zs, y):
        for q in range(self.chunks):
            p = self.part(zs, y, 1 - self.c, q)
            remote(
                p, p, self.s_c.at[zs, y, q], self.r_c.at[zs, y, q], blk=self.y * 2 + 1 - self.c
            ).wait_recv()

    def drain(self):
        @pl.loop(0, self.nz)
        def _(zs):
            for q in range(self.chunks):

                @pl.when(self.goes_right(zs))
                def _():
                    self.right(zs, q).wait_send()

                @pl.when(self.goes_left(zs))
                def _():
                    self.left(zs, q).wait_send()

                self.across(zs, q).wait_send()
                self.sibling(zs, 0, q).wait_send()
                self.sibling(zs, 1, q).wait_send()


class DpGather:
    def __init__(self, buf, sems, nz, n_dp):
        self.d, self.n_dp, self.nz, self.buf = lax.axis_index("dp"), n_dp, nz, buf
        self.s_x, self.r_x, self.s_f, self.r_f = sems[:4]
        self.plane = Gather(buf, sems[4:], nz, (self.d,), 1)
        self.z, self.y, self.c = position()

    def to_dp(self, zs, y, r):
        p = self.buf.at[self.d, zs, y, self.c]
        sems = self.s_x.at[zs, y, r], self.r_x.at[zs, y, r]
        return remote(p, p, *sems, dp=(self.d + r) % self.n_dp)

    def relay(self, zs, y, c, r, sems):
        p = self.buf.at[(self.d + self.n_dp - r) % self.n_dp, zs, y, c]
        sems = (sem.at[zs, y, r] for sem in sems)
        return remote(p, p, *sems, blk=self.y * 2 + 1 - self.c)

    def row_step(self, n):
        self.plane.row_step(n)
        self.send_on(by_distance(self.z, n, self.nz), self.y)

    def cross_step(self, n):
        self.plane.cross_step(n)
        self.send_on(by_distance(self.z, n, self.nz), 1 - self.y)

    def send_on(self, zs, y):
        @pl.loop(1, self.n_dp)
        def _(r):
            self.to_dp(zs, y, r).start()

    def each(self, act):
        @pl.loop(0, self.nz)
        def _(n):
            zs = by_distance(self.z, n, self.nz)
            for y in (self.y, 1 - self.y):

                @pl.loop(1, self.n_dp)
                def _(r):
                    act(zs, y, r)

    def finish(self):
        def pass_on(zs, y, r):
            self.relay(zs, y, self.c, r, (self.s_x, self.r_x)).wait_recv()
            self.relay(zs, y, self.c, r, (self.s_f, self.r_f)).start()

        def end(zs, y, r):
            self.relay(zs, y, 1 - self.c, r, (self.s_f, self.r_f)).wait_recv()
            self.relay(zs, y, self.c, r, (self.s_f, self.r_f)).wait_send()
            self.to_dp(zs, y, r).wait_send()

        self.each(pass_on)

        @pl.loop(0, self.nz)
        def _(zs):
            self.plane.ready(zs, 0)
            self.plane.ready(zs, 1)

        self.each(end)
        self.plane.drain()


def dp_gather_sems(nz, n_dp):
    return [pltpu.SemaphoreType.DMA((nz, 2, n_dp)) for _ in range(4)] + gather_sems(nz, 1)


def scatter_sems(nz):
    return [pltpu.SemaphoreType.DMA((nz * CHUNKS,)) for _ in range(7)]


def scatter_buffers(nz, rows, width):
    two, one = pltpu.VMEM((nz, 2, rows, width), BF16), pltpu.VMEM((nz, rows, width), BF16)
    return [two, two, one, pltpu.VMEM((nz + 1, rows, width), BF16)]


class Scatter:
    def __init__(self, theirs, bufs, sems, nz):
        self.theirs, self.nz = theirs, nz
        self.mine, self.rc, self.ry, self.rz = bufs
        self.s_c, self.r_c, self.s_y, self.r_y, self.s_z, self.r_l, self.r_r = sems
        self.z, self.y, self.c = position()
        self.rows = self.mine.shape[2] // CHUNKS
        self.units = nz * CHUNKS
        self.steps = self.units + nz + 1

    def place(self, k):
        r = k % (2 * CHUNKS)
        pair = k // (2 * CHUNKS)
        return jnp.where(r % 2 == 0, self.nz - 1 - pair, pair), r // 2

    def unit(self, k):
        zs, q = self.place(k)
        return zs, pl.ds(q * self.rows, self.rows)

    def to_sibling(self, k):
        zs, part = self.unit(k)
        return remote(
            self.theirs(zs, part), self.rc.at[zs, :, part, :], self.s_c.at[k], self.r_c.at[k],
            blk=self.y * 2 + 1 - self.c,
        )

    def across(self, k):
        zs, part = self.unit(k)
        return remote(
            self.mine.at[zs, 1 - self.y, part, :], self.ry.at[zs, part, :],
            self.s_y.at[k], self.r_y.at[k], blk=(1 - self.y) * 2 + self.c,
        )

    def right(self, k):
        zs, part = self.unit(k)
        return remote(
            self.mine.at[zs, self.y, part, :], self.rz.at[zs, part, :],
            self.s_z.at[k], self.r_l.at[k], hs=self.z + 1,
        )

    def left(self, k):
        zs, part = self.unit(k)
        place = jnp.where(zs == self.z - 1, self.nz, zs)
        return remote(
            self.mine.at[zs, self.y, part, :], self.rz.at[place, part, :],
            self.s_z.at[k], self.r_r.at[k], hs=self.z - 1,
        )

    def take(self, buf, sem, k, place=None):
        zs, part = self.unit(k)
        place = zs if place is None else place
        p = buf.at[place, part, :]
        remote(p, p, self.s_z.at[k], sem.at[k], blk=self.y * 2 + 1 - self.c).wait_recv()
        return buf[place, part, :].astype(F32)

    def add(self, k, row, other):
        zs, part = self.unit(k)
        self.mine[zs, row, part, :] = (self.mine[zs, row, part, :].astype(F32) + other).astype(
            BF16
        )

    def chip_sum(self, k):
        zs, part = self.unit(k)
        self.to_sibling(k).wait_recv()
        self.add(k, 1 - self.y, self.rc[zs, 1 - self.y, part, :].astype(F32))
        self.across(k).start()
        self.add(k, self.y, self.rc[zs, self.y, part, :].astype(F32))

    def row_sum(self, k):
        self.add(k, self.y, self.take(self.ry, self.r_y, k))

    def pass_on(self, k, buf, sem, start, first):
        @pl.when(jnp.logical_not(first))
        def _():
            self.add(k, self.y, self.take(buf, sem, k))

        start(k).start()

    def finish(self, k, out_ref):
        zs, part = self.unit(k)
        out_ref[part, :] = self.mine[zs, self.y, part, :].astype(F32)

        @pl.when(self.z > 0)
        def _():
            out_ref[part, :] += self.take(self.rz, self.r_l, k)

        @pl.when(self.z < self.nz - 1)
        def _():
            out_ref[part, :] += self.take(self.rz, self.r_r, k, self.nz)

    def step(self, k, out_ref):
        @pl.when(k < self.units)
        def _():
            self.chip_sum(k)

        self.later(k, out_ref)

    def later(self, k, out_ref):
        z, nz = self.z, self.nz

        def valid(m):
            return jnp.logical_and(m >= 0, m < self.units)

        @pl.when(valid(k - 1))
        def _():
            self.row_sum(k - 1)

        m = k - 1 - z

        @pl.when(jnp.logical_and(valid(m), self.unit(m)[0] > z))
        def _():
            self.pass_on(m, self.rz, self.r_l, self.right, z == 0)

        w = k - 1 - (nz - 1 - z)

        @pl.when(jnp.logical_and(valid(w), self.unit(w)[0] < z))
        def _():
            self.pass_on(w, self.rz, self.r_r, self.left, z == nz - 1)

        f = k - 1 - jnp.maximum(z, nz - 1 - z)

        @pl.when(jnp.logical_and(valid(f), self.unit(f)[0] == z))
        def _():
            self.finish(f, out_ref)

    def drain(self):
        @pl.loop(0, self.units)
        def _(k):
            self.to_sibling(k).wait_send()
            self.across(k).wait_send()

            @pl.when(self.unit(k)[0] > self.z)
            def _():
                self.right(k).wait_send()

            @pl.when(self.unit(k)[0] < self.z)
            def _():
                self.left(k).wait_send()


def exchange_sems(nz):
    dma = pltpu.SemaphoreType.DMA
    return [dma((nz * 4,)), dma((nz * 4,)), dma]


class Exchange:
    def __init__(self, src, dst, sems, nz):
        self.src, self.dst = src, dst
        self.send, self.recv, self.own = sems
        self.peers = nz * 4
        z, y, c = position()
        self.me = z * 4 + y * 2 + c

    def copy(self, r):
        t = (self.me + r) % self.peers
        return remote(
            self.src(t), self.dst(self.me), self.send.at[r], self.recv.at[r],
            hs=t // 4, blk=t % 4,
        )

    def arrival(self, r):
        t = (self.me + self.peers - r) % self.peers
        p = self.dst(t)
        return remote(p, p, self.send.at[r], self.recv.at[r], hs=t // 4, blk=t % 4)

    def keep(self):
        return pltpu.make_async_copy(self.src(self.me), self.dst(self.me), self.own)

    def start(self):
        self.keep().start()

        @pl.loop(1, self.peers)
        def _(r):
            self.copy(r).start()

    def arrive(self):
        self.keep().wait()

        @pl.loop(1, self.peers)
        def _(r):
            self.arrival(r).wait_recv()

    def drain(self):
        @pl.loop(1, self.peers)
        def _(r):
            self.copy(r).wait_send()


def attn_fwd_kernel(
    nz, n_dp, block, tile, slot_ref, order_ref, qkv_ref, base_ref, step_ref, cot_ref, wm_ref,
    q_out, k_out, v_out, ctxt_out, lse_out, ctx_out, cot_all, wm_in,
    qm, vt, ctx_sorted, ctx_blocks, ctx_slots, g, own_sem, o_cot, s_x, r_x, *sems,
):
    gather = Gather(g, sems[3:], nz)
    z, y, c = gather.z, gather.y, gather.c
    d = lax.axis_index("dp")
    own = pltpu.make_async_copy(cot_ref, g.at[z, y, c], own_sem)
    own.start()

    def x_copy(r):
        return remote(
            wm_ref, wm_in.at[r - 1], s_x.at[r], r_x.at[r], dp=(d + r) % n_dp
        )

    def cot_copy(zs, yy):
        return pltpu.make_async_copy(g.at[zs, yy], cot_all.at[zs, yy], o_cot.at[zs, yy])
    moves = Exchange(
        lambda t: ctx_slots.at[t],
        lambda t: ctx_out.at[:, pl.ds(pl.multiple_of(t * 2 * HEAD_DIM, 128), 2 * HEAD_DIM)],
        sems[:3],
        nz,
    )
    greet_all(nz, n_dp)
    own.wait()
    gather.row_step(0)

    @pl.loop(1, n_dp)
    def _(r):
        x_copy(r).start()

    length = q_out.shape[0]
    width = 2 * HEAD_DIM
    n_blocks = length // block
    n_tiles = length // tile

    @pl.loop(0, n_blocks)
    def _(b):
        dst = pl.ds(pl.multiple_of(b * block, block), block)
        cos, sin = rope_of_block(base_ref, step_ref, b)
        qkv = qkv_ref[slot_ref[b]]
        q = qkv[:, 0:width]
        k = qkv[:, width : 2 * width]
        v = qkv[:, 2 * width : 3 * width]
        q = (q * cos + swap_halves(q) * sin).astype(BF16)
        k = (k * cos + swap_halves(k) * sin).astype(BF16)
        q_out[dst, :] = q
        k_out[dst, :] = k
        v_out[dst, :] = v.astype(BF16)
        low = lax.broadcasted_iota(jnp.int32, q.shape, 1) < HEAD_DIM
        zero = jnp.zeros_like(q)
        qm[0, dst, :] = jnp.where(low, q, zero)
        qm[1, dst, :] = jnp.where(low, zero, q)

    @pl.loop(0, n_tiles)
    def _(t):
        rows = pl.ds(pl.multiple_of(t * tile, tile), tile)
        both = v_out[rows, :].astype(F32).T.astype(BF16)
        for h in range(2):
            vt[h, 0:HEAD_DIM, rows] = both[h * HEAD_DIM : (h + 1) * HEAD_DIM, :]
            vt[h, HEAD_DIM:, rows] = jnp.ones((16, tile), BF16)

    diag = lax.broadcasted_iota(jnp.int32, (tile, tile), 0) <= lax.broadcasted_iota(
        jnp.int32, (tile, tile), 1
    )

    @pl.loop(0, n_tiles)
    def _(i):
        rows_q = pl.ds(pl.multiple_of(i * tile, tile), tile)
        queries = [qm[0, rows_q, :], qm[1, rows_q, :]]

        def step(j, carry, masked):
            rows_k = pl.ds(pl.multiple_of(j * tile, tile), tile)
            keys = k_out[rows_k, :]
            new = []
            for h in range(2):
                top, acc = carry[h]
                s = dot_nt(keys, queries[h]) * EXP2_SCALE
                if masked:
                    s = jnp.where(diag, s, -1e30)
                new_top = jnp.maximum(top, jnp.max(s, axis=0, keepdims=True))
                p = jnp.exp2(s - new_top).astype(BF16)
                acc = acc * jnp.exp2(top - new_top) + dot_nn(vt[h, :, rows_k], p)
                new.append((new_top, acc))
            return tuple(new)

        start = tuple(
            (jnp.full((1, tile), -1e30, F32), jnp.zeros((HEAD_DIM + 16, tile), F32))
            for _ in range(2)
        )
        carry = lax.fori_loop(0, i, lambda j, c: step(j, c, False), start)
        carry = step(i, carry, True)
        outs = []
        for h in range(2):
            top, acc = carry[h]
            total = acc[HEAD_DIM : HEAD_DIM + 1, :]
            outs.append(acc[0:HEAD_DIM, :] / total)
            lse_out[h : h + 1, rows_q] = top + jnp.log2(total)
        both = jnp.concatenate(outs, axis=0)
        ctxt_out[:, rows_q] = both
        ctx_sorted[rows_q, :] = both.T.astype(BF16)

        for e, at in ((2, 5), (3, 3), (4, 2), (5, 1)):

            @pl.when(i == n_tiles - at)
            def _():
                gather.chunk_step(e)

    @pl.loop(0, n_blocks)
    def _(b):
        ctx_blocks[b] = ctx_sorted[pl.ds(pl.multiple_of(b * block, block), block), :]

    @pl.loop(0, n_blocks)
    def _(t):
        ctx_slots[t] = ctx_blocks[order_ref[t]]

    moves.start()

    @pl.loop(6, nz * CHUNKS + CHUNKS)
    def _(e):
        gather.chunk_step(e)

    @pl.loop(0, nz)
    def _(n):
        zs = by_distance(z, n, nz)
        for yy in (y, 1 - y):
            gather.ready(zs, yy)
            cot_copy(zs, yy).start()

    moves.arrive()
    moves.drain()
    gather.drain()

    @pl.loop(0, nz)
    def _(zs):
        for yy in range(2):
            cot_copy(zs, yy).wait()

    @pl.loop(1, n_dp)
    def _(r):
        x_copy(r).wait()


def attn_fwd(slot_of_block, order, qkv, base, step, cot, wm, nz, n_dp, tile):
    length = qkv.shape[0]
    width = 2 * HEAD_DIM
    block, wide = cot.shape
    whole = pl.BlockSpec(memory_space=pltpu.VMEM)
    smem = pl.BlockSpec(memory_space=pltpu.SMEM)
    any_spec = pl.BlockSpec(memory_space=pl.ANY)
    *rest, cot_all, wm_in = pl.pallas_call(
        functools.partial(attn_fwd_kernel, nz, n_dp, block, tile),
        in_specs=[smem, smem, whole, whole, whole, any_spec, any_spec],
        out_specs=[whole] * 5 + [any_spec] * 3,
        out_shape=[
            jax.ShapeDtypeStruct((length, width), BF16),
            jax.ShapeDtypeStruct((length, width), BF16),
            jax.ShapeDtypeStruct((length, width), BF16),
            jax.ShapeDtypeStruct((width, length), F32),
            jax.ShapeDtypeStruct((2, length), F32),
            jax.ShapeDtypeStruct((block, wide), BF16),
            jax.ShapeDtypeStruct((nz, 2, 2, block, wide), BF16),
            jax.ShapeDtypeStruct((max(n_dp - 1, 1),) + wm.shape, BF16),
        ],
        scratch_shapes=[
            pltpu.VMEM((2, length, width), BF16),
            pltpu.VMEM((2, HEAD_DIM + 16, length), BF16),
            pltpu.VMEM((length, width), BF16),
            pltpu.VMEM((length // block, block, width), BF16),
            pltpu.VMEM((length // block, block, width), BF16),
            pltpu.VMEM((nz, 2, 2, block, wide), BF16),
            pltpu.SemaphoreType.DMA,
            pltpu.SemaphoreType.DMA((nz, 2)),
            pltpu.SemaphoreType.DMA((n_dp,)),
            pltpu.SemaphoreType.DMA((n_dp,)),
        ]
        + exchange_sems(nz)
        + gather_sems(nz),
        compiler_params=pltpu.CompilerParams(
            vmem_limit_bytes=VMEM_LIMIT, collective_id=5, has_side_effects=True
        ),
        cost_estimate=pl.CostEstimate(
            flops=20 * length * length * HEAD_DIM,
            bytes_accessed=30 * length * wide,
            transcendentals=length * length,
        ),
        name="attn_fwd",
    )(slot_of_block, order, qkv.reshape(length // block, block, -1), base, step, cot, wm)
    return *rest, cot_all.reshape(length, wide), wm_in


def attn_bwd_kernel(
    nz, n_dp, block, tile,
    slot_ref, order_ref, q_ref, k_ref, v_ref, dctx_ref, ctxt_ref, lse_ref, base_ref, step_ref, p_ref, go_ref, xn_ref,
    out_ref, sum_ref, go_in, gq_ref,
    qm, dom, do_slots, do_sorted, kt, delta, dqt, dk_buf, dv_buf, d_blocks, acc, x_buf, l_x, l_m, s_x, r_x, *rest,
):
    bufs, sems = rest[:4], rest[4:]
    sc = Scatter(lambda zs, part: p_ref.at[zs, :, 1 - sc.c, part, :], bufs, sems[3:], nz)
    moves = Exchange(
        lambda t: dctx_ref.at[:, pl.ds(pl.multiple_of(t * 2 * HEAD_DIM, 128), 2 * HEAD_DIM)],
        lambda t: do_slots.at[t],
        sems[:3],
        nz,
    )

    def load(k):
        zs, part = sc.unit(k)
        return pltpu.make_async_copy(
            p_ref.at[zs, :, sc.c, part, :], bufs[0].at[zs, :, part, :], l_m.at[k]
        )

    d = lax.axis_index("dp")

    def x_copy(r):
        t = (d + r) % n_dp
        return remote(go_ref.at[t], go_in.at[r], s_x.at[r], r_x.at[r], dp=t)

    greet_all(nz, n_dp)
    moves.start()

    @pl.loop(1, n_dp)
    def _(r):
        x_copy(r).start()

    @pl.loop(0, sc.units)
    def _(k):
        sc.to_sibling(k).start()
        load(k).start()

    @pl.loop(0, sc.units)
    def _(k):
        load(k).wait()
        sc.chip_sum(k)

    moves.arrive()
    length = q_ref.shape[0]
    width = 2 * HEAD_DIM
    n_blocks = length // block
    n_tiles = length // tile
    scale = HEAD_DIM**-0.5

    @pl.loop(0, n_blocks)
    def _(b):
        dst = pl.ds(pl.multiple_of(b * block, block), block)
        do_sorted[dst, :] = do_slots[slot_ref[b]]

    @pl.loop(0, n_tiles)
    def _(t):
        rows = pl.ds(pl.multiple_of(t * tile, tile), tile)
        low = lax.broadcasted_iota(jnp.int32, (tile, width), 1) < HEAD_DIM
        q = q_ref[rows, :]
        do = do_sorted[rows, :]
        zero = jnp.zeros_like(q)
        qm[0, rows, :] = jnp.where(low, q, zero)
        qm[1, rows, :] = jnp.where(low, zero, q)
        dom[0, rows, :] = jnp.where(low, do, zero)
        dom[1, rows, :] = jnp.where(low, zero, do)
        kt[:, rows] = k_ref[rows, :].astype(F32).T.astype(BF16)
        prod = do.astype(F32).T * ctxt_ref[:, rows]
        delta[0:1, rows] = jnp.sum(prod[0:HEAD_DIM, :], axis=0, keepdims=True)
        delta[1:2, rows] = jnp.sum(prod[HEAD_DIM:, :], axis=0, keepdims=True)
        dqt[:, rows] = jnp.zeros((width, tile), F32)

    diag = lax.broadcasted_iota(jnp.int32, (tile, tile), 0) <= lax.broadcasted_iota(
        jnp.int32, (tile, tile), 1
    )

    @pl.loop(0, n_tiles)
    def _(j):
        sc.later(j + 1, sum_ref)
        rows_k = pl.ds(pl.multiple_of(j * tile, tile), tile)
        keys = k_ref[rows_k, :]
        vals = v_ref[rows_k, :]

        def step(i, carry, masked):
            rows_q = pl.ds(pl.multiple_of(i * tile, tile), tile)
            dk, dv = carry
            for h in range(2):
                s = dot_nt(keys, qm[h, rows_q, :]) * EXP2_SCALE
                p = jnp.exp2(s - lse_ref[h : h + 1, rows_q])
                if masked:
                    p = jnp.where(diag, p, 0.0)
                dp = dot_nt(vals, dom[h, rows_q, :])
                ds = (p * (dp - delta[h : h + 1, rows_q])).astype(BF16)
                dv = dv + dot_nn(p.astype(BF16), dom[h, rows_q, :])
                dk = dk + dot_nn(ds, qm[h, rows_q, :])
                part = slice(h * HEAD_DIM, (h + 1) * HEAD_DIM)
                dqt[part, rows_q] += dot_nn(kt[part, rows_k], ds)
            return dk, dv

        zero = jnp.zeros((tile, width), F32)
        carry = step(j, (zero, zero), True)
        dk, dv = lax.fori_loop(j + 1, n_tiles, lambda i, c: step(i, c, False), carry)
        dk_buf[rows_k, :] = (dk * scale).astype(BF16)
        dv_buf[rows_k, :] = dv.astype(BF16)

    @pl.loop(0, n_tiles)
    def _(t):
        rows = pl.ds(pl.multiple_of(t * tile, tile), tile)
        do_sorted[rows, :] = (dqt[:, rows].T * scale).astype(BF16)

    @pl.loop(0, n_blocks)
    def _(b):
        src = pl.ds(pl.multiple_of(b * block, block), block)
        cos, sin = rope_of_block(base_ref, step_ref, b)
        dq = do_sorted[src, :].astype(F32)
        dk = dk_buf[src, :].astype(F32)
        d_blocks[b, :, 0:width] = (dq * cos - swap_halves(dq) * sin).astype(BF16)
        d_blocks[b, :, width : 2 * width] = (dk * cos - swap_halves(dk) * sin).astype(BF16)
        d_blocks[b, :, 2 * width : 3 * width] = dv_buf[src, :]

    @pl.loop(0, n_blocks)
    def _(t):
        out_ref[t] = d_blocks[order_ref[t]]

    def x_load(p):
        return pltpu.make_async_copy(xn_ref.at[p], x_buf.at[p % 2], l_x.at[p % 2])

    pairs = xn_ref.shape[0]
    x_load(0).start()
    acc[...] = jnp.zeros_like(acc)

    @pl.loop(n_tiles + 1, sc.steps)
    def _(k):
        for j in range(2):
            p = 2 * (k - n_tiles - 1) + j

            @pl.when(p < pairs)
            def _():
                @pl.when(p + 1 < pairs)
                def _():
                    x_load(p + 1).start()

                x_load(p).wait()
                d_pair = out_ref[pl.ds(2 * p, 2)].reshape(2 * block, 3 * width)
                acc[...] += dot_tn(x_buf[p % 2], d_pair)

        sc.later(k, sum_ref)

    gq_ref[...] = acc[...].astype(BF16)
    moves.drain()
    sc.drain()

    @pl.loop(1, n_dp)
    def _(r):
        x_copy(r).wait()


def attn_bwd(
    slot_of_block, order, q, k, v, d_ctx, ctxt, lse, base, step, partial, grad_out, xn, nz, tile
):
    length, width = q.shape
    block, wide = d_ctx.shape
    whole = pl.BlockSpec(memory_space=pltpu.VMEM)
    smem = pl.BlockSpec(memory_space=pltpu.SMEM)
    any_spec = pl.BlockSpec(memory_space=pl.ANY)
    n_dp = grad_out.shape[0]
    d_qkv, summed, grad_out_in, grad_qkv = pl.pallas_call(
        functools.partial(attn_bwd_kernel, nz, n_dp, block, tile),
        in_specs=[smem, smem] + [whole] * 3 + [any_spec] + [whole] * 4 + [any_spec] * 3,
        out_specs=[whole, whole, any_spec, whole],
        out_shape=[
            jax.ShapeDtypeStruct((length // block, block, 3 * width), BF16),
            jax.ShapeDtypeStruct((block, wide), F32),
            jax.ShapeDtypeStruct(grad_out.shape, BF16),
            jax.ShapeDtypeStruct((wide, 3 * width), BF16),
        ],
        scratch_shapes=[
            pltpu.VMEM((2, length, width), BF16),
            pltpu.VMEM((2, length, width), BF16),
            pltpu.VMEM((length // block, block, width), BF16),
            pltpu.VMEM((length, width), BF16),
            pltpu.VMEM((width, length), BF16),
            pltpu.VMEM((2, length), F32),
            pltpu.VMEM((width, length), F32),
            pltpu.VMEM((length, width), BF16),
            pltpu.VMEM((length, width), BF16),
            pltpu.VMEM((length // block, block, 3 * width), BF16),
            pltpu.VMEM((wide, 3 * width), F32),
            pltpu.VMEM((2, 2 * block, wide), BF16),
            pltpu.SemaphoreType.DMA((2,)),
            pltpu.SemaphoreType.DMA((nz * CHUNKS,)),
            pltpu.SemaphoreType.DMA((n_dp,)),
            pltpu.SemaphoreType.DMA((n_dp,)),
        ]
        + scatter_buffers(nz, block, wide)
        + exchange_sems(nz)
        + scatter_sems(nz),
        compiler_params=pltpu.CompilerParams(
            vmem_limit_bytes=VMEM_LIMIT, collective_id=6, has_side_effects=True
        ),
        cost_estimate=pl.CostEstimate(
            flops=50 * length * length * HEAD_DIM,
            bytes_accessed=60 * length * wide,
            transcendentals=length * length,
        ),
        name="attn_bwd",
    )(
        slot_of_block, order, q, k, v, d_ctx, ctxt, lse, base, step,
        partial.reshape(nz, 2, 2, block, wide), grad_out, xn.reshape(2 * nz, 2 * block, wide),
    )
    return d_qkv.reshape(length, 3 * width), summed, grad_out_in, grad_qkv


def scatter_mlp_kernel(
    nz, p_ref, x_ref, c_ref, dgu_ref, hid_ref,
    out_ref, grad_ref,
    acc, x_buf, c_buf, dgu_buf, hid_buf, l_m, l_x, l_c, l_g, l_h, *rest,
):
    bufs, sems = rest[:4], rest[4:]
    mine = bufs[0]
    pairs = x_ref.shape[0]
    gate_up = dgu_ref.shape[2]
    tile = 512 if acc.shape[0] % 512 == 0 else acc.shape[0]

    sc = Scatter(lambda zs, part: p_ref.at[zs, :, 1 - sc.c, part, :], bufs, sems, nz)

    def load(k):
        zs, part = sc.unit(k)
        return pltpu.make_async_copy(
            p_ref.at[zs, :, sc.c, part, :], mine.at[zs, :, part, :], l_m.at[k]
        )

    def operands(k):
        s = k % 2
        return [
            pltpu.make_async_copy(ref.at[k], buf.at[s], sem.at[s])
            for ref, buf, sem in (
                (x_ref, x_buf, l_x),
                (c_ref, c_buf, l_c),
                (dgu_ref, dgu_buf, l_g),
                (hid_ref, hid_buf, l_h),
            )
        ]

    greet_neighbours(nz)

    @pl.loop(0, sc.units)
    def _(k):
        sc.to_sibling(k).start()
        load(k).start()

    for copy in operands(0):
        copy.start()
    acc[...] = jnp.zeros_like(acc)

    def weight_grads(k):
        @pl.when(k + 1 < pairs)
        def _():
            for copy in operands(k + 1):
                copy.start()

        for copy in operands(k):
            copy.wait()
        s = k % 2

        @pl.loop(0, acc.shape[0] // tile)
        def _(t):
            at = pl.ds(pl.multiple_of(t * tile, tile), tile)
            acc[at, 0:gate_up] += dot_tn(x_buf[s, :, at], dgu_buf[s])
            acc[at, gate_up:] += dot_tn(c_buf[s, :, at], hid_buf[s])

    @pl.loop(0, sc.steps)
    def _(k):
        @pl.when(k < sc.units)
        def _():
            load(k).wait()

        sc.step(k, out_ref)

        @pl.when(k < pairs)
        def _():
            weight_grads(k)

    grad_ref[...] = acc[...].astype(BF16)
    sc.drain()


def scatter_mlp(partial, x_all, c_all, d_gu, hid, nz, collective_id):
    rows, width = partial.shape[0] // (nz * 4), partial.shape[1]
    hidden = hid.shape[1]
    pairs = 2 * nz
    any_spec = pl.BlockSpec(memory_space=pl.ANY)
    vmem = pl.BlockSpec(memory_space=pltpu.VMEM)
    dma = pltpu.SemaphoreType.DMA

    def by_pair(a):
        return a.reshape(pairs, 2 * rows, a.shape[1])

    def buffers(cols):
        return pltpu.VMEM((2, 2 * rows, cols), BF16)

    return pl.pallas_call(
        functools.partial(scatter_mlp_kernel, nz),
        in_specs=[any_spec] * 5,
        out_specs=[vmem, vmem],
        out_shape=[
            jax.ShapeDtypeStruct((rows, width), F32),
            jax.ShapeDtypeStruct((width, 3 * hidden), BF16),
        ],
        scratch_shapes=[
            pltpu.VMEM((width, 3 * hidden), F32),
            buffers(width),
            buffers(width),
            buffers(2 * hidden),
            buffers(hidden),
            dma((nz * CHUNKS,)),
            dma((2,)),
            dma((2,)),
            dma((2,)),
            dma((2,)),
        ]
        + scatter_buffers(nz, rows, width)
        + scatter_sems(nz),
        compiler_params=pltpu.CompilerParams(
            vmem_limit_bytes=VMEM_LIMIT, collective_id=collective_id, has_side_effects=True
        ),
        cost_estimate=pl.CostEstimate(
            flops=6 * partial.size * hidden,
            bytes_accessed=60 * partial.size,
            transcendentals=0,
        ),
        name="scatter_mlp",
    )(
        partial.reshape(nz, 2, 2, rows, width),
        by_pair(x_all),
        by_pair(c_all),
        by_pair(d_gu),
        by_pair(hid),
    )


def scatter_last_kernel(
    nz, n_dp, dq_ref, w_ref, gq_ref, gm_ref, go_ref, go_in,
    out_ref, gq_out, gm_out,
    theirs, gq_in, gq_sum, gm_in, gm_sum, go_buf,
    l_o, l_q, s_xq, r_xq, own_q, s_q, r_q, l_m, s_xm, r_xm, own_m, s_m, r_m, *rest,
):
    bufs, sems = rest[:4], rest[4:]
    sc = Scatter(lambda zs, part: theirs.at[zs, :, part, :], bufs, sems, nz)
    mine = bufs[0]
    d = lax.axis_index("dp")
    rows, width = dq_ref.shape[3], mine.shape[3]
    shard = gq_in.shape[2]
    cols = dq_ref.shape[4]
    gq_moves = Exchange(
        lambda t: gq_sum.at[t], lambda t: gq_out.at[t], (s_q, r_q, own_q), nz
    )
    gm_moves = Exchange(
        lambda t: gm_sum.at[t], lambda t: gm_out.at[t], (s_m, r_m, own_m), nz
    )

    keep_q = pltpu.make_async_copy(gq_ref.at[d], gq_in.at[0], l_q)
    keep_q.start()
    keep_m = pltpu.make_async_copy(gm_ref.at[d], gm_sum, l_m)
    keep_m.start()

    def xq_copy(r):
        t = (d + r) % n_dp
        return remote(gq_ref.at[t], gq_in.at[r], s_xq.at[r], r_xq.at[r], dp=t)

    def xm_copy(i, r):
        t = (gm_moves.me + i) % gm_moves.peers
        dp = (d + r) % n_dp
        return remote(gm_ref.at[dp, t], gm_in.at[r - 1, t], s_xm.at[i, r], r_xm.at[i, r], dp=dp)

    greet_all(nz, n_dp)

    @pl.loop(1, n_dp)
    def _(r):
        xq_copy(r).start()

        @pl.loop(1, gm_moves.peers + 1)
        def _(i):
            xm_copy(i, r).start()

    def partial_sums(zs, core):
        left = dq_ref[zs, :, core].reshape(2 * rows, cols)
        return dot_nt(left, w_ref[:, 0:cols]).astype(BF16).reshape(2, rows, width)

    def out_loads(zs):
        own = pltpu.make_async_copy(go_ref.at[d, zs], go_buf.at[0], l_o.at[0])
        return [own] + [
            pltpu.make_async_copy(go_in.at[r, zs], go_buf.at[r], l_o.at[r]) for r in range(1, n_dp)
        ]

    def out_sums(core):
        return sum(go_buf[r, :, core].astype(F32) for r in range(n_dp)).astype(BF16)

    if mine.shape[2] > rows + shard:
        for buf in (mine, theirs):
            buf[:, :, rows + shard :, :] = jnp.zeros_like(buf[:, :, rows + shard :, :])

    def produce(i):
        zs = jnp.where(i % 2 == 0, nz - 1 - i // 2, i // 2)
        for copy in out_loads(zs):
            copy.start()
        theirs[zs, :, 0:rows, :] = partial_sums(zs, 1 - sc.c)
        for copy in out_loads(zs):
            copy.wait()
        theirs[zs, :, rows : rows + shard, :] = out_sums(1 - sc.c)
        for q in range(CHUNKS):
            sc.to_sibling(2 * CHUNKS * (i // 2) + 2 * q + i % 2).start()
        mine[zs, :, 0:rows, :] = partial_sums(zs, sc.c)
        mine[zs, :, rows : rows + shard, :] = out_sums(sc.c)

    @pl.loop(0, 2)
    def _(i):
        produce(i)

    keep_m.wait()

    def mlp_block(i):
        t = (gm_moves.me + i) % gm_moves.peers
        @pl.loop(1, n_dp)
        def _(r):
            xm_copy(i, r).wait_recv()
            gm_sum[t] = (gm_sum[t].astype(F32) + gm_in[r - 1, t].astype(F32)).astype(BF16)

        @pl.when(i < gm_moves.peers)
        def _():
            gm_moves.copy(i).start()

        @pl.when(i == gm_moves.peers)
        def _():
            gm_moves.keep().start()

    @pl.loop(0, sc.steps)
    def _(k):
        sc.step(k, out_ref)

        @pl.when(k < nz - 2)
        def _():
            produce(k + 2)

        @pl.when(k == 1)
        def _():
            keep_q.wait()
            gq_sum[...] = gq_in[0]

            @pl.loop(1, n_dp)
            def _(r):
                xq_copy(r).wait_recv()
                gq_sum[...] = (gq_sum[...].astype(F32) + gq_in[r].astype(F32)).astype(BF16)

            gq_moves.start()

        for j in range(2):
            i = 2 * (k - 2) + 1 + j

            @pl.when(jnp.logical_and(i >= 1, i <= gm_moves.peers))
            def _():
                mlp_block(i)

    sc.drain()
    for moves in (gq_moves, gm_moves):
        moves.arrive()
        moves.drain()

    @pl.loop(1, n_dp)
    def _(r):
        xq_copy(r).wait_send()

        @pl.loop(1, gm_moves.peers + 1)
        def _(i):
            xm_copy(i, r).wait_send()


def scatter_last(d_qkv, w, grad_qkv, grad_mlp, grad_out, grad_out_in, nz, n_dp, collective_id):
    peers = nz * 4
    rows, cols = d_qkv.shape[0] // peers, d_qkv.shape[1]
    width = w.shape[0]
    shard = width // (n_dp * peers)
    cols_mlp = grad_mlp.shape[1]
    all_rows = rows + max(shard, 16 * CHUNKS)
    any_spec = pl.BlockSpec(memory_space=pl.ANY)
    vmem = pl.BlockSpec(memory_space=pltpu.VMEM)
    dma = pltpu.SemaphoreType.DMA
    return pl.pallas_call(
        functools.partial(scatter_last_kernel, nz, n_dp),
        in_specs=[vmem, vmem] + [any_spec] * 4,
        out_specs=[vmem, any_spec, any_spec],
        out_shape=[
            jax.ShapeDtypeStruct((all_rows, width), F32),
            jax.ShapeDtypeStruct((peers, shard, cols), BF16),
            jax.ShapeDtypeStruct((peers, shard, cols_mlp), BF16),
        ],
        scratch_shapes=[
            pltpu.VMEM((nz, 2, all_rows, width), BF16),
            pltpu.VMEM((n_dp, peers, shard, cols), BF16),
            pltpu.VMEM((peers, shard, cols), BF16),
            pltpu.VMEM((n_dp - 1, peers, shard, cols_mlp), BF16),
            pltpu.VMEM((peers, shard, cols_mlp), BF16),
            pltpu.VMEM((n_dp, 2, 2, shard, width), BF16),
            dma((n_dp,)),
            dma,
            dma((n_dp,)),
            dma((n_dp,)),
            dma,
            dma((peers,)),
            dma((peers,)),
            dma,
            dma((peers + 1, n_dp)),
            dma((peers + 1, n_dp)),
            dma,
            dma((peers,)),
            dma((peers,)),
        ]
        + scatter_buffers(nz, all_rows, width)
        + scatter_sems(nz),
        compiler_params=pltpu.CompilerParams(
            vmem_limit_bytes=VMEM_LIMIT, collective_id=collective_id, has_side_effects=True
        ),
        cost_estimate=pl.CostEstimate(
            flops=2 * peers * rows * width * cols,
            bytes_accessed=60 * peers * rows * width,
            transcendentals=0,
        ),
        name="scatter_last",
    )(
        d_qkv.reshape(nz, 2, 2, rows, cols),
        w,
        grad_qkv.reshape(n_dp, peers, shard, cols),
        grad_mlp.reshape(n_dp, peers, shard, cols_mlp),
        grad_out.reshape(n_dp, nz, 2, 2, shard, width),
        grad_out_in.reshape(n_dp, nz, 2, 2, shard, width),
    )


def layout_kernel(
    gq_ref, gm_ref, wq_ref, wgu_ref, g1_ref, g2_ref, q_out, gu_out, down_out, g1_out, g2_out
):
    peers = gq_ref.shape[0]
    part_q = gq_ref.shape[2] // 3
    hid = gm_ref.shape[2] // 3
    sum_q = jnp.zeros((gq_ref.shape[1], part_q), F32)
    sum_m = jnp.zeros((gq_ref.shape[1], hid), F32)
    for t in range(peers):
        for s in range(3):
            at = pl.ds((s * peers + t) * part_q, part_q)
            block = gq_ref[t, :, s * part_q : (s + 1) * part_q].astype(F32)
            q_out[:, at] = block
            sum_q += block * wq_ref[:, at].astype(F32)
        for s in range(2):
            at = pl.ds((s * peers + t) * hid, hid)
            block = gm_ref[t, :, s * hid : (s + 1) * hid].astype(F32)
            gu_out[:, at] = block
            sum_m += block * wgu_ref[:, at].astype(F32)
        down_out[:, t * hid : (t + 1) * hid] = gm_ref[t, :, 2 * hid :].astype(F32)
    g1_out[...] = jnp.sum(sum_q, axis=1, keepdims=True) / g1_ref[...].astype(F32)
    g2_out[...] = jnp.sum(sum_m, axis=1, keepdims=True) / g2_ref[...].astype(F32)


def layout_call(grad_qkv, grad_mlp, w_qkv, w_gate_up, gain_one, gain_two):
    shard = w_qkv.shape[0]
    hidden = w_gate_up.shape[1] // 2
    vmem = pl.BlockSpec(memory_space=pltpu.VMEM)
    return pl.pallas_call(
        layout_kernel,
        in_specs=[vmem] * 6,
        out_specs=[vmem] * 5,
        out_shape=[
            jax.ShapeDtypeStruct(w_qkv.shape, F32),
            jax.ShapeDtypeStruct(w_gate_up.shape, F32),
            jax.ShapeDtypeStruct((shard, hidden), F32),
            jax.ShapeDtypeStruct((shard, 1), F32),
            jax.ShapeDtypeStruct((shard, 1), F32),
        ],
        compiler_params=pltpu.CompilerParams(vmem_limit_bytes=VMEM_LIMIT),
        name="layout",
    )(grad_qkv, grad_mlp, w_qkv, w_gate_up, gain_one[:, None], gain_two[:, None])


def gather_qkv_kernel(
    nz, n_dp, tok_ref, wq_ref, wgu_ref, wd_ref, wo_ref,
    xn_ref, qkv_ref, gain_ref, wq_out, wm_out, wo_out,
    g, wq, xn_stage, own_sem, s_w, r_w, s_d, r_d, s_m, r_m, own_w, own_m, own_o, o_xn, o_w,
    *sems,
):
    peers = nz * 4
    gather = Gather(g, sems[:7], nz)
    w_out = DpGather(wo_out, sems[7:], nz, n_dp)
    z, y, c = gather.z, gather.y, gather.c
    me = z * 4 + y * 2 + c
    d = lax.axis_index("dp")
    pair_rows = 2 * tok_ref.shape[0]
    cols = qkv_ref.shape[2]
    shard = wq_ref.shape[1]
    hid = wd_ref.shape[1] // peers

    def block_rows(dp, t):
        return pl.ds(pl.multiple_of((dp * peers + t) * shard, shard), shard)

    def plane_rows(dp):
        return pl.ds(pl.multiple_of(dp * (peers * shard), peers * shard), peers * shard)

    def mlp_part(t, s):
        first = t * hid if s != 1 else (peers + t) * hid
        cols_t = pl.ds(pl.multiple_of(first, hid), hid)
        return (wd_ref if s == 2 else wgu_ref).at[:, cols_t]

    def mlp_place(t, s):
        return wm_out.at[block_rows(0, t), pl.ds(s * hid, hid)]

    own = pltpu.make_async_copy(tok_ref, g.at[z, y, c], own_sem)
    own.start()
    keep_w = pltpu.make_async_copy(wq_ref.at[me], wq.at[block_rows(d, me), :], own_w)
    keep_w.start()
    keep_o = pltpu.make_async_copy(wo_ref, wo_out.at[d, z, y, c], own_o)
    keep_o.start()
    keep_m = [
        pltpu.make_async_copy(mlp_part(me, s), mlp_place(me, s), own_m.at[s]) for s in range(3)
    ]
    for copy in keep_m:
        copy.start()

    greet_all(nz, n_dp)

    def place(t):
        return {"hs": t // 4, "blk": t % 4}

    def w_copy(r):
        t = (me + r) % peers
        return remote(
            wq_ref.at[t], wq.at[block_rows(d, me), :], s_w.at[r], r_w.at[r], **place(t)
        )

    def w_take(r):
        t = (me + peers - r) % peers
        p = wq.at[block_rows(d, t), :]
        return remote(p, p, s_w.at[r], r_w.at[r], **place(t))

    def m_copy(r, s):
        t = (me + r) % peers
        return remote(
            mlp_part(t, s), mlp_place(me, s), s_m.at[r, s], r_m.at[r, s], **place(t)
        )

    def m_take(r, s):
        t = (me + peers - r) % peers
        p = mlp_place(t, s)
        return remote(p, p, s_m.at[r, s], r_m.at[r, s], **place(t))

    def d_copy(r):
        p = wq.at[plane_rows(d), :]
        return remote(p, p, s_d.at[r], r_d.at[r], dp=(d + r) % n_dp)

    def d_take(r):
        p = wq.at[plane_rows((d + n_dp - r) % n_dp), :]
        return remote(p, p, s_d.at[r], r_d.at[r], dp=(d + r) % n_dp)

    def mlp_sends(first, last):
        @pl.loop(first, last)
        def _(r):
            for s in range(3):
                m_copy(r, s).start()

    own.wait()
    gather.row_step(0)

    @pl.loop(1, peers)
    def _(r):
        w_copy(r).start()

    keep_o.wait()
    w_out.row_step(0)
    third = peers // 3
    mlp_sends(1, 1 + third)
    gather.row_step(1)
    gather.cross_step(0)
    mlp_sends(1 + third, 1 + 2 * third)
    w_out.row_step(1)
    w_out.cross_step(0)

    @pl.loop(1, peers)
    def _(r):
        w_take(r).wait_recv()

    keep_w.wait()

    @pl.loop(1, n_dp)
    def _(r):
        d_copy(r).start()

    @pl.loop(2, nz)
    def _(n):
        gather.row_step(n)
        gather.cross_step(n - 1)

        @pl.when(n == 2)
        def _():
            mlp_sends(1 + 2 * third, peers)

        w_out.row_step(n)
        w_out.cross_step(n - 1)

    @pl.loop(1, n_dp)
    def _(r):
        d_take(r).wait_recv()

    gain_ref[...] = wq[:, cols:].astype(F32).T[0:8, :]
    keep_out = pltpu.make_async_copy(wq, wq_out, o_w)
    keep_out.start()
    gain = gain_ref[0:1, :]

    def xn_copy(m, pair):
        return pltpu.make_async_copy(xn_stage.at[m % 2], xn_ref.at[pair], o_xn.at[m % 2])

    @pl.loop(0, 2 * nz)
    def _(m):
        zs = by_distance(z, m // 2, nz)
        yy = jnp.where(m % 2 == 0, y, 1 - y)
        pair = zs * 2 + yy

        @pl.when(m == 2 * nz - 1)
        def _():
            gather.cross_step(nz - 1)
            w_out.cross_step(nz - 1)

        gather.ready(zs, yy)

        @pl.when(m >= 2)
        def _():
            xn_copy(m, pair).wait()

        x = g[zs, yy].reshape(pair_rows, g.shape[4]).astype(F32)
        xn = rms_scale(x, gain).astype(BF16)
        xn_stage[m % 2] = xn
        xn_copy(m, pair).start()
        qkv_ref[pair] = dot_nn(xn, wq[:, 0:cols])

    w_out.finish()
    for m in range(2):
        xn_copy(m, 0).wait()
    gather.drain()
    keep_out.wait()

    @pl.loop(1, peers)
    def _(r):
        w_copy(r).wait_send()
        for s in range(3):
            m_copy(r, s).wait_send()
            m_take(r, s).wait_recv()

    for copy in keep_m:
        copy.wait()

    @pl.loop(1, n_dp)
    def _(r):
        d_copy(r).wait_send()


def gather_qkv(tokens, wq_parts, w_gate_up, w_down, w_out, nz, n_dp, cols):
    rows, width = tokens.shape
    peers, shard, wide = wq_parts.shape
    hid = w_down.shape[1] // peers
    any_spec = pl.BlockSpec(memory_space=pl.ANY)
    vmem = pl.BlockSpec(memory_space=pltpu.VMEM)
    dma = pltpu.SemaphoreType.DMA
    length = peers * rows
    xn, qkv, gains, wq, wm, wo = pl.pallas_call(
        functools.partial(gather_qkv_kernel, nz, n_dp),
        in_specs=[any_spec] * 5,
        out_specs=[any_spec, vmem, vmem, any_spec, any_spec, any_spec],
        out_shape=[
            jax.ShapeDtypeStruct((peers // 2, 2 * rows, width), BF16),
            jax.ShapeDtypeStruct((peers // 2, 2 * rows, cols), F32),
            jax.ShapeDtypeStruct((8, width), F32),
            jax.ShapeDtypeStruct((width, wide), BF16),
            jax.ShapeDtypeStruct((width // n_dp, 3 * hid), BF16),
            jax.ShapeDtypeStruct((n_dp, nz, 2, 2, shard, width), BF16),
        ],
        scratch_shapes=[
            pltpu.VMEM((nz, 2, 2, rows, width), BF16),
            pltpu.VMEM((n_dp * peers * shard, wide), BF16),
            pltpu.VMEM((2, 2 * rows, width), BF16),
            dma,
            dma((peers,)),
            dma((peers,)),
            dma((n_dp,)),
            dma((n_dp,)),
            dma((peers, 3)),
            dma((peers, 3)),
            dma,
            dma((3,)),
            dma,
            dma((2,)),
            dma,
        ]
        + gather_sems(nz)
        + dp_gather_sems(nz, n_dp),
        compiler_params=pltpu.CompilerParams(
            vmem_limit_bytes=VMEM_LIMIT, collective_id=1, has_side_effects=True
        ),
        cost_estimate=pl.CostEstimate(
            flops=2 * length * width * cols,
            bytes_accessed=60 * length * width,
            transcendentals=0,
        ),
        name="gather_qkv",
    )(tokens, wq_parts, w_gate_up, w_down, w_out)
    return (
        xn.reshape(length, width), qkv.reshape(length, cols), gains, wq, wm,
        wo.reshape(width, width),
    )


def gather_mlp_kernel(
    nz, n_dp, x_ref, c_ref, wm_ref, wm_in,
    xn_ref, out_ref, dx_ref, hid_ref, dgu_ref,
    g, w_ref, c_buf, out_buf, dx_buf, hid_buf, dgu_buf,
    w_sem, own_sem, c_sem, x_sem, out_sem, dx_sem, hid_sem, dgu_sem, *sems,
):
    gather = Gather(g, sems, nz)
    z, y, c = gather.z, gather.y, gather.c
    hidden = w_ref.shape[1] // 3
    w_gate, w_up, w_down = (pl.ds(i * hidden, hidden) for i in range(3))
    pair_rows = 2 * x_ref.shape[0]
    steps = 2 * nz

    own = pltpu.make_async_copy(x_ref, g.at[z, y, c], own_sem)
    own.start()
    d = lax.axis_index("dp")
    half = wm_ref.shape[0]

    def w_load(r):
        start = pl.multiple_of(((d + n_dp - r) % n_dp) * half, half)
        src = wm_ref if r == 0 else wm_in.at[r - 1]
        return pltpu.make_async_copy(src, w_ref.at[pl.ds(start, half), :], w_sem.at[r])

    for r in range(n_dp):
        w_load(r).start()

    def place(m):
        return by_distance(z, m // 2, nz), jnp.where(m % 2 == 0, y, 1 - y)

    def pair(m):
        zs, yy = place(m)
        return zs * 2 + yy

    def c_copy(m):
        return pltpu.make_async_copy(c_ref.at[pair(m)], c_buf.at[m % 2], c_sem.at[m % 2])

    def x_copy(m):
        zs, yy = place(m)
        return pltpu.make_async_copy(g.at[zs, yy], xn_ref.at[zs, yy], x_sem.at[m])

    def results(m):
        s = m % 2
        return [
            pltpu.make_async_copy(buf.at[s], ref.at[pair(m)], sem.at[s])
            for buf, ref, sem in (
                (out_buf, out_ref, out_sem),
                (dx_buf, dx_ref, dx_sem),
                (hid_buf, hid_ref, hid_sem),
                (dgu_buf, dgu_ref, dgu_sem),
            )
        ]

    c_copy(0).start()
    greet_neighbours(nz)
    own.wait()
    gather.row_step(0)
    for r in range(n_dp):
        w_load(r).wait()

    @pl.loop(0, steps)
    def _(m):
        @pl.when(m % 2 == 1)
        def _():
            n = (m + 1) // 2

            @pl.when(n < nz)
            def _():
                gather.row_step(n)

            gather.cross_step(n - 1)

        zs, yy = place(m)
        gather.ready(zs, yy)
        x_copy(m).start()

        @pl.when(m + 1 < steps)
        def _():
            c_copy(m + 1).start()

        @pl.when(m >= 2)
        def _():
            for copy in results(m - 2):
                copy.wait()

        c_copy(m).wait()
        s = m % 2
        x = g[zs, yy].reshape(pair_rows, g.shape[4])
        gate = dot_nn(x, w_ref[:, w_gate])
        up = dot_nn(x, w_ref[:, w_up])
        d_hid = dot_nn(c_buf[s], w_ref[:, w_down])
        sigma = 1.0 / (1.0 + jnp.exp(-gate))
        act = gate * sigma
        hid = (act * up).astype(BF16)
        d_gate = (d_hid * up * (sigma * (1.0 + gate * (1.0 - sigma)))).astype(BF16)
        d_up = (d_hid * act).astype(BF16)
        hid_buf[s] = hid
        dgu_buf[s, :, 0:hidden] = d_gate
        dgu_buf[s, :, hidden:] = d_up
        dx = dot_nt(d_gate, w_ref[:, w_gate]) + dot_nt(d_up, w_ref[:, w_up])
        dx_buf[s] = dx.astype(BF16)
        out_buf[s] = dot_nt(hid, w_ref[:, w_down]).astype(BF16)
        for copy in results(m):
            copy.start()

    for m in (steps - 2, steps - 1):
        for copy in results(m):
            copy.wait()

    @pl.loop(0, steps)
    def _(m):
        x_copy(m).wait()

    gather.drain()


def gather_mlp(xn, c_all, wm, wm_in, nz, n_dp):
    rows, width = xn.shape
    hidden = wm.shape[1] // 3
    pairs = nz * 2
    length = 2 * pairs * rows
    any_spec = pl.BlockSpec(memory_space=pl.ANY)
    dma = pltpu.SemaphoreType.DMA

    def by_pair(cols):
        return jax.ShapeDtypeStruct((pairs, 2 * rows, cols), BF16)

    def buffers(cols):
        return pltpu.VMEM((2, 2 * rows, cols), BF16)

    xn_all, out_part, dx_part, hid, d_gu = pl.pallas_call(
        functools.partial(gather_mlp_kernel, nz, n_dp),
        in_specs=[any_spec] * 4,
        out_specs=[any_spec] * 5,
        out_shape=[
            jax.ShapeDtypeStruct((nz, 2, 2, rows, width), BF16),
            by_pair(width),
            by_pair(width),
            by_pair(hidden),
            by_pair(2 * hidden),
        ],
        scratch_shapes=[
            pltpu.VMEM((nz, 2, 2, rows, width), BF16),
            pltpu.VMEM((width, 3 * hidden), BF16),
            buffers(width),
            buffers(width),
            buffers(width),
            buffers(hidden),
            buffers(2 * hidden),
            dma((n_dp,)),
            dma,
            dma((2,)),
            dma((pairs,)),
            dma((2,)),
            dma((2,)),
            dma((2,)),
            dma((2,)),
        ]
        + gather_sems(nz),
        compiler_params=pltpu.CompilerParams(
            vmem_limit_bytes=VMEM_LIMIT, collective_id=2, has_side_effects=True
        ),
        cost_estimate=pl.CostEstimate(
            flops=12 * length * width * hidden,
            bytes_accessed=60 * length * width,
            transcendentals=length * hidden,
        ),
        name="gather_mlp",
    )(xn, c_all.reshape(pairs, 2 * rows, width), wm, wm_in)
    return (
        xn_all.reshape(length, width),
        out_part.reshape(length, width),
        dx_part.reshape(length, width),
        hid.reshape(length, hidden),
        d_gu.reshape(length, 2 * hidden),
    )


def by_group(weight, groups, sections):
    rows, cols = weight.shape
    part = cols // (groups * sections)
    parts = weight.reshape(rows, sections, groups, part)
    return jnp.transpose(parts, (2, 0, 1, 3)).reshape(groups, rows, sections * part)


def body(tokens, block_order, gain_attn, w_qkv, w_out, gain_mlp, w_gate_up, w_down, cotangent):
    nz = lax.axis_size("hs")
    groups = nz * lax.axis_size("blk")
    n_dp = lax.axis_size("dp")
    tok_rows, width = tokens.shape
    shard = w_qkv.shape[0]
    length = groups * tok_rows

    order = block_order[0]
    slot_of_block = jnp.argsort(order).astype(jnp.int32)
    base, step = rope_tables(groups, tok_rows)

    gain_columns = jnp.pad(jnp.stack([gain_attn, gain_mlp], axis=1), ((0, 0), (0, 126)))
    wq_parts = jnp.concatenate(
        [
            by_group(w_qkv, groups, 3),
            jnp.broadcast_to(gain_columns[None], (groups,) + gain_columns.shape),
        ],
        axis=2,
    )
    xn1_all, qkv, gains, wqkv_mine, wmlp_mine, wout_full = gather_qkv(
        tokens, wq_parts, w_gate_up, w_down, w_out, nz, n_dp, 3 * width // groups
    )

    q, k, v, ctxt, lse, ctx_tok, cot_all, wmlp_other = attn_fwd(
        slot_of_block, order, qkv, base, step, cotangent, wmlp_mine, nz, n_dp, 512
    )

    x_float = tokens.astype(F32)
    gain_one, gain_two = gains[0], gains[1]
    y_mid = x_float + dot_nn(ctx_tok, wout_full)
    xn2 = rms_scale(y_mid, gain_two).astype(BF16)

    xn2_all, out_part, dx_part, hid, d_gu = gather_mlp(
        xn2, cot_all, wmlp_mine, wmlp_other, nz, n_dp
    )
    d_xn2, grad_mlp = scatter_mlp(dx_part, xn2_all, cot_all, d_gu, hid, nz, 3)
    _, pull_two = jax.vjp(lambda v: rms_scale(v, gain_two), y_mid)
    (dy_norm,) = pull_two(d_xn2)
    d_mid = cotangent.astype(F32) + dy_norm
    d_mid_b = d_mid.astype(BF16)

    d_ctx = dot_nt(d_mid_b, wout_full).astype(BF16)
    grad_out = dot_tn(ctx_tok, d_mid_b).astype(BF16).reshape(n_dp, groups * shard, width)

    d_qkv, mlp_out, grad_out_in, grad_qkv = attn_bwd(
        slot_of_block, order, q, k, v, d_ctx, ctxt, lse, base, step, out_part, grad_out, xn1_all,
        nz, 512,
    )
    layer_out = (y_mid + mlp_out).astype(BF16)
    sums, grad_qkv, grad_mlp = scatter_last(
        d_qkv, wqkv_mine, grad_qkv, grad_mlp, grad_out, grad_out_in, nz, n_dp, 4
    )
    d_xn1, out_rows = sums[:tok_rows], sums[tok_rows : tok_rows + shard]
    qkv_rows, gu_rows, down_rows, grad_gain_one, grad_gain_two = layout_call(
        grad_qkv, grad_mlp, w_qkv, w_gate_up, gain_attn, gain_mlp
    )

    _, pull_one = jax.vjp(lambda v: rms_scale(v, gain_one), x_float)
    (dx_norm,) = pull_one(d_xn1)
    grad_tokens = d_mid + dx_norm
    return (
        layer_out,
        grad_tokens,
        grad_gain_one.reshape(shard),
        qkv_rows,
        out_rows,
        grad_gain_two.reshape(shard),
        gu_rows,
        down_rows,
    )


def solution(mesh):
    rows = P(ALL, None)
    in_specs = (rows, P("dp", None), P(ALL), rows, rows, P(ALL), rows, rows, rows)
    out_specs = (rows, rows, P(ALL), rows, rows, P(ALL), rows, rows)
    return jax.shard_map(body, mesh=mesh, in_specs=in_specs, out_specs=out_specs, check_vma=False)
```

time: 3830 us -> 801 us (0.21)
  waiting for transfers between devices: 2730 us -> 0 us
  Pallas kernels: 0 us -> 755 us
  matrix products: 494 us -> 15 us
  other arithmetic: 250 us -> 17.7 us
  blocking collectives: 188 us -> 0 us
  local copies, waits for them, and re-layouts: 120 us -> 5.67 us
    reduce_scatter x3 -> x0, waiting for transfers between devices: 2070 us -> none  [the longest x1 1600 us: body(): lax.psum_scatter(jnp.concatenate([contract_rows(left_a, d_gate_up), contr...]
    pallas_call x0 -> x7, Pallas kernels: none -> 755 us  [the longest x1 188 us: scatter_last(): pl.pallas_call(functools.partial(scatter_last_kernel, nz, n_dp), in_specs...]
    all_gather x5 -> x0, waiting for transfers between devices: 553 us -> none  [the longest x1 233 us: body(): lax.all_gather(w_gate_up, ('dp', 'hs', 'blk'), axis=0, tiled=True)]
    dot_general x40 -> x3, matrix products: 494 us -> 15 us  [the longest x1 5.6 us: dot_tn(): lax.dot_general(a, b, (((0,), (0,)), ((), ())), preferred_element_type=F32)]
    concatenate x6 -> x1, other arithmetic: 179 us -> 1.09 us  [body(): jnp.concatenate([by_group(w_qkv, groups, 3), jnp.broadcast_to(gain_column...]
    all_to_all x3 -> x0, waiting for transfers between devices: 113 us -> none  [the longest x1 58.9 us: body(): lax.all_to_all(d_packed, 'hs', split_axis=0, concat_axis=2, tiled=True)]
    all_to_all x1 -> x0, blocking collectives: 98.9 us -> none  [body(): lax.all_to_all(packed, 'hs', split_axis=2, concat_axis=0, tiled=True)]
    unnamed x2 -> x0, blocking collectives: 89.1 us -> none
  transfers between devices with their start and end apart: 11 -> 0, of which waited for: 10 -> 0; matrix products, arithmetic and copies ran while one was open for 12% -> 0% of each run, Pallas kernels for 0% -> 0%
where the time goes in v1:
time: 801 us; the launch traced here: 794 us
  Pallas kernels  755 us (94%)
  other arithmetic  17.7 us (2%)
  matrix products  15 us (2%)
    pallas_call x1, Pallas kernels, scatter_last(): pl.pallas_call(functools.partial(scatter_last_kernel, nz, n_dp), in_specs...  188 us
    pallas_call x1, Pallas kernels, gather_qkv(): pl.pallas_call(functools.partial(gather_qkv_kernel, nz, n_dp), in_specs=[...  166 us
    pallas_call x1, Pallas kernels, attn_bwd(): pl.pallas_call(functools.partial(attn_bwd_kernel, nz, n_dp, block, tile),...  113 us
    pallas_call x1, Pallas kernels, scatter_mlp(): pl.pallas_call(functools.partial(scatter_mlp_kernel, nz), in_specs=[any_s...  100 us
    pallas_call x1, Pallas kernels, attn_fwd(): pl.pallas_call(functools.partial(attn_fwd_kernel, nz, n_dp, block, tile),...  99.1 us
    pallas_call x1, Pallas kernels, gather_mlp(): pl.pallas_call(functools.partial(gather_mlp_kernel, nz, n_dp), in_specs=[...  82.3 us

profile of v1, /device:TPU:13, one launch (start us, length us, event | category | flops | bytes accessed | tf_op | source)
XLA Modules:
  0.0 794.4 jit_solution(14533638264220751168)
XLA Ops:
  0.7 1.2 broadcast_multiply_fusion.1
  1.8 0.8 pad_maximum_fusion.1.step_ref
  2.6 0.7 pad_maximum_fusion.3
  3.6 0.5 copy.30
  4.1 0.7 reshape.388
  4.8 1.1 pad_maximum_fusion.wq_ref
  5.9 166.1 %gather_qkv.1 = (bf16[8,384,2048]{2,1,0:T(8,128)(2,1)}, f32[8,384,384]{2,1,0:T(8,128)}, f32[8,2048]{1,0:T(8,128)}, bf16[2048,512]{1,0:T(8,128)(2,1)}, bf16[1024,...) custom-call(bf16[192,2048]{1,0:T(8,128)(2,1)} %tok_ref.1, bf16[16,64,512]{2,1,0:T(8,128)(2,1)} %pad_maximum_fusion.wq_ref, ...), custom_call_target="tpu_custom_call" | custom-call | flops 4831838208 | bytes 377487360 | tf_op jit(solution)/shard_map/gather_qkv/pallas_call | solution.py:1473
  172.0 0.1 multiply_cosine_fusion.1
  172.2 0.6 pad_maximum_fusion.2.base_ref
  172.8 1.2 sort.17
  174.0 99.1 %attn_fwd.1 = (bf16[3072,128]{1,0:T(8,128)(2,1)}, bf16[3072,128]{1,0:T(8,128)(2,1)}, bf16[3072,128]{1,0:T(8,128)(2,1)}, f32[128,3072]{1,0:T(8,128)}, f32[2,3072]...) custom-call(s32[16]{0:T(128)} %get-tuple-element.42.slot_ref, ...), custom_call_target="tpu_custom_call" | custom-call | flops 12079595520 | bytes 188743680 | tf_op jit(solution)/shard_map/attn_fwd/pallas_call | solution.py:662
  273.2 5.6 multiply_reduce_fusion.1
  278.8 0.9 fusion.8
  279.7 1.1 multiply_convert_fusion.x_ref
  280.8 82.3 %gather_mlp.1 = (bf16[4,2,2,192,2048]{4,3,2,1,0:T(8,128)(2,1)}, bf16[8,384,2048]{2,1,0:T(8,128)(2,1)}, bf16[8,384,2048]{2,1,0:T(8,128)(2,1)}, bf16[8,384,512]{2,1,0:T(8,128)(2,1)}, bf16[8,384,1024]{2,1,0:T(8,128)(2,1)}) custom-call(bf16[192,2048]{1,0:T(8,128)(2,1)} %multiply_convert_fusion.x_ref, bf16[8,384,2048]{2,1,0:T(8,128)(2,1)} %bitcast.49, ...), custom_call_target="tpu_custom_call" | custom-call | flops 38654705664 | bytes 377487360 | tf_op jit(solution)/shard_map/gather_mlp/pallas_call | solution.py:1649
  363.1 100.2 %scatter_mlp.1 = (f32[192,2048]{1,0:T(8,128)}, bf16[2048,1536]{1,0:T(8,128)(2,1)}) custom-call(bf16[4,2,2,192,2048]{4,3,2,1,0:T(8,128)(2,1)} %bitcast.52, bf16[8,384,2048]{2,1,0:T(8,128)(2,1)} %bitcast.51, bf16[8,384,2048]{2,1,0:T(8,128)(2,1)} %bitcast.50, bf16[8,384,1024]{2,1,0:T(8,128)(2,1)} %get-tuple-element.55.dgu_ref, ...), custom_call_target="tpu_custom_call" | custom-call | flops 19327352832 | bytes 377487360 | tf_op jit(solution)/shard_map/scatter_mlp/pallas_call | solution.py:1005
  463.3 1.8 multiply_reduce_fusion
  465.2 0.2 copy-done.5
  465.4 0.5 fusion
  465.9 0.6 copy-done.4
  466.5 5.6 convolution_convert_fusion
  472.2 3.8 convolution_convert_fusion.1.dctx_ref
  475.9 112.8 %attn_bwd.1 = (bf16[16,192,384]{2,1,0:T(8,128)(2,1)}, f32[192,2048]{1,0:T(8,128)}, bf16[2,1024,2048]{2,1,0:T(8,128)(2,1)}, bf16[2048,384]{1,0:T(8,128)(2,1)}) custom-call(s32[16]{0:T(128)} %get-tuple-element.42.slot_ref, s32[16]{0:T(128)} %bitcast.46, bf16[3072,128]{1,0:T(8,128)(2,1)} %get-tuple-element.47.q_ref, bf16[3072,128]{1,0:T(8,128)(2,1)} %get-tuple-element.48.k_ref, ...), custom_call_target="tpu_custom_call" | custom-call | flops 30198988800 | bytes 377487360 | tf_op jit(solution)/shard_map/attn_bwd/pallas_call | solution.py:870
  588.8 187.5 %scatter_last.1 = (f32[256,2048]{1,0:T(8,128)}, bf16[16,64,384]{2,1,0:T(8,128)(2,1)}, bf16[16,64,1536]{2,1,0:T(8,128)(2,1)}) custom-call(bf16[4,2,2,192,384]{4,3,2,1,0:T(8,128)(2,1)} %bitcast.34, bf16[2048,512]{1,0:T(8,128)(2,1)} %get-tuple-element.64.w_ref, bf16[2,16,64,384]{3,2,1,0:T(8,128)(2,1)} %bitcast.35, bf16[2,16,64,1536]{3,2,1,0:T(8,128)(2,1)} %bitcast.30, ...), custom_call_target="tpu_custom_call" | custom-call | flops 4831838208 | bytes 377487360 | tf_op jit(solution)/shard_map/scatter_last/pallas_call | solution.py:1191
  776.4 0.7 copy.25.g1_ref
  777.1 0.7 copy.26.g2_ref
  777.8 6.6 layout.1
  784.4 1.4 reduce
  785.8 1.4 reduce.1
  787.2 2.2 fusion.2
  789.5 3.7 fusion.1
  793.2 0.8 slice.15
  (33 shorter events, 0.5 us)
Async XLA Ops:
  0.6 2.8 copy-start.3
  5.9 166.1 %copy-start.6 = (f32[128]{0:T(128)S(1)}, f32[128]{0:T(128)}, u32[]{:S(2)}) copy-start(f32[128]{0:T(128)} %constant.34) | copy-start | bytes 1540
  5.9 166.9 %copy-start.9 = (s32[1,16]{1,0:T(1,128)S(1)}, s32[1,16]{1,0:T(1,128)}, u32[]{:S(2)}) copy-start(s32[1,16]{1,0:T(1,128)} %param.12) | copy-start | bytes 196
  174.0 99.1 %copy-start.2 = (bf16[192,2048]{1,0:T(8,128)(2,1)S(1)}, bf16[192,2048]{1,0:T(8,128)(2,1)}, u32[]{:S(2)}) copy-start(bf16[192,2048]{1,0:T(8,128)(2,1)} %tok_ref.1) | copy-start | bytes 2359300
  463.3 1.9 copy-start.1
  463.3 2.1 copy-start.5
  465.4 1.1 copy-start.4
  465.4 6.7 slice-start
  466.5 5.6 slice-start.1
  588.8 187.6 %copy-start.7 = (bf16[64]{0:T(256)(128)(2,1)S(1)}, bf16[64]{0:T(256)(128)(2,1)}, u32[]{:S(2)}) copy-start(bf16[64]{0:T(256)(128)(2,1)} %param.13) | copy-start | bytes 388
  588.8 188.3 %copy-start.8 = (bf16[64]{0:T(256)(128)(2,1)S(1)}, bf16[64]{0:T(256)(128)(2,1)}, u32[]{:S(2)}) copy-start(bf16[64]{0:T(256)(128)(2,1)} %param.16) | copy-start | bytes 388
  787.2 2.3 copy-start

commit v2 on v1

--- a/solution.py
+++ b/solution.py
@@ -73,6 +73,7 @@
 
 MESH = pl.DeviceIdType.MESH
 CHUNKS = 2
+FINE = 4
 
 
 def position():
@@ -311,8 +312,8 @@
     return [pltpu.SemaphoreType.DMA((nz, 2, n_dp)) for _ in range(4)] + gather_sems(nz, 1)
 
 
-def scatter_sems(nz):
-    return [pltpu.SemaphoreType.DMA((nz * CHUNKS,)) for _ in range(7)]
+def scatter_sems(nz, chunks=CHUNKS):
+    return [pltpu.SemaphoreType.DMA((nz * chunks,)) for _ in range(7)]
 
 
 def scatter_buffers(nz, rows, width):
@@ -321,18 +322,18 @@
 
 
 class Scatter:
-    def __init__(self, theirs, bufs, sems, nz):
-        self.theirs, self.nz = theirs, nz
+    def __init__(self, theirs, bufs, sems, nz, chunks=CHUNKS):
+        self.theirs, self.nz, self.chunks = theirs, nz, chunks
         self.mine, self.rc, self.ry, self.rz = bufs
         self.s_c, self.r_c, self.s_y, self.r_y, self.s_z, self.r_l, self.r_r = sems
         self.z, self.y, self.c = position()
-        self.rows = self.mine.shape[2] // CHUNKS
-        self.units = nz * CHUNKS
+        self.rows = self.mine.shape[2] // chunks
+        self.units = nz * chunks
         self.steps = self.units + nz + 1
 
     def place(self, k):
-        r = k % (2 * CHUNKS)
-        pair = k // (2 * CHUNKS)
+        r = k % (2 * self.chunks)
+        pair = k // (2 * self.chunks)
         return jnp.where(r % 2 == 0, self.nz - 1 - pair, pair), r // 2
 
     def unit(self, k):
@@ -410,13 +411,6 @@
         def _():
             out_ref[part, :] += self.take(self.rz, self.r_r, k, self.nz)
 
-    def step(self, k, out_ref):
-        @pl.when(k < self.units)
-        def _():
-            self.chip_sum(k)
-
-        self.later(k, out_ref)
-
     def later(self, k, out_ref):
         z, nz = self.z, self.nz
 
@@ -508,12 +502,108 @@
             self.copy(r).wait_send()
 
 
+def outermost(i, nz):
+    return jnp.where(i % 2 == 0, nz - 1 - i // 2, i // 2)
+
+
+def early_blocks(peers):
+    return peers // 4
+
+
+def mlp_block_sems(nz, n_dp, count):
+    dma = pltpu.SemaphoreType.DMA
+    return [dma((count,)), dma((count, n_dp)), dma((count, n_dp))] + exchange_sems(nz)
+
+
+class MlpBlocks:
+    def __init__(self, parts, arrived, summed, out, sems, nz, n_dp, first, count):
+        self.l_m, self.s_x, self.r_x = sems[:3]
+        self.parts, self.arrived, self.summed, self.n_dp = parts, arrived, summed, n_dp
+        self.peers = nz * 4
+        self.first, self.last = first, first + count
+        self.d = lax.axis_index("dp")
+        self.moves = Exchange(
+            lambda t: summed.at[(t - self.me + self.peers - 1) % self.peers + 1 - first],
+            lambda t: out.at[t],
+            sems[3:],
+            nz,
+        )
+        self.me = self.moves.me
+
+    def each(self, act):
+        @pl.loop(self.first, self.last)
+        def _(i):
+            act(i)
+
+    def each_dp(self, act):
+        @pl.loop(1, self.n_dp)
+        def _(r):
+            act(r)
+
+    def own(self, i):
+        k = i - self.first
+        t = (self.me + i) % self.peers
+        return pltpu.make_async_copy(
+            self.parts.at[self.d, t], self.summed.at[k], self.l_m.at[k]
+        )
+
+    def x_copy(self, i, r):
+        k = i - self.first
+        t = (self.me + i) % self.peers
+        dp = (self.d + r) % self.n_dp
+        return remote(
+            self.parts.at[dp, t], self.arrived.at[r - 1, k],
+            self.s_x.at[k, r], self.r_x.at[k, r], dp=dp,
+        )
+
+    def load(self):
+        self.each(lambda i: self.own(i).start())
+
+    def start(self):
+        self.each(lambda i: self.each_dp(lambda r: self.x_copy(i, r).start()))
+
+    def add(self, i):
+        k = i - self.first
+        self.own(i).wait()
+
+        def one(r):
+            self.x_copy(i, r).wait_recv()
+            self.summed[k] = (
+                self.summed[k].astype(F32) + self.arrived[r - 1, k].astype(F32)
+            ).astype(BF16)
+
+        self.each_dp(one)
+
+        @pl.when(i < self.peers)
+        def _():
+            self.moves.copy(i).start()
+
+        @pl.when(i == self.peers)
+        def _():
+            self.moves.keep().start()
+
+    def finish(self):
+        def end(i):
+            @pl.when(i < self.peers)
+            def _():
+                self.moves.copy(i).wait_send()
+                self.moves.arrival(i).wait_recv()
+
+            @pl.when(i == self.peers)
+            def _():
+                self.moves.keep().wait()
+
+            self.each_dp(lambda r: self.x_copy(i, r).wait_send())
+
+        self.each(end)
+
+
 def attn_fwd_kernel(
     nz, n_dp, block, tile, slot_ref, order_ref, qkv_ref, base_ref, step_ref, cot_ref, wm_ref,
     q_out, k_out, v_out, ctxt_out, lse_out, ctx_out, cot_all, wm_in,
     qm, vt, ctx_sorted, ctx_blocks, ctx_slots, g, own_sem, o_cot, s_x, r_x, *sems,
 ):
-    gather = Gather(g, sems[3:], nz)
+    gather = Gather(g, sems[3:], nz, chunks=FINE)
     z, y, c = gather.z, gather.y, gather.c
     d = lax.axis_index("dp")
     own = pltpu.make_async_copy(cot_ref, g.at[z, y, c], own_sem)
@@ -574,6 +664,8 @@
     diag = lax.broadcasted_iota(jnp.int32, (tile, tile), 0) <= lax.broadcasted_iota(
         jnp.int32, (tile, tile), 1
     )
+    early = {6: [0], 5: [1], 4: [2], 3: [3], 2: [4, 5], 1: [6, 7]}
+    early = {at: [FINE + e for e in events] for at, events in early.items()}
 
     @pl.loop(0, n_tiles)
     def _(i):
@@ -611,11 +703,12 @@
         ctxt_out[:, rows_q] = both
         ctx_sorted[rows_q, :] = both.T.astype(BF16)
 
-        for e, at in ((2, 5), (3, 3), (4, 2), (5, 1)):
+        for at, events in early.items():
 
             @pl.when(i == n_tiles - at)
             def _():
-                gather.chunk_step(e)
+                for e in events:
+                    gather.chunk_step(e)
 
     @pl.loop(0, n_blocks)
     def _(b):
@@ -627,7 +720,7 @@
 
     moves.start()
 
-    @pl.loop(6, nz * CHUNKS + CHUNKS)
+    @pl.loop(FINE + 8, nz * FINE + FINE)
     def _(e):
         gather.chunk_step(e)
 
@@ -686,7 +779,7 @@
             pltpu.SemaphoreType.DMA((n_dp,)),
         ]
         + exchange_sems(nz)
-        + gather_sems(nz),
+        + gather_sems(nz, FINE),
         compiler_params=pltpu.CompilerParams(
             vmem_limit_bytes=VMEM_LIMIT, collective_id=5, has_side_effects=True
         ),
@@ -702,12 +795,15 @@
 
 def attn_bwd_kernel(
     nz, n_dp, block, tile,
-    slot_ref, order_ref, q_ref, k_ref, v_ref, dctx_ref, ctxt_ref, lse_ref, base_ref, step_ref, p_ref, go_ref, xn_ref,
-    out_ref, sum_ref, go_in, gq_ref,
-    qm, dom, do_slots, do_sorted, kt, delta, dqt, dk_buf, dv_buf, d_blocks, acc, x_buf, l_x, l_m, s_x, r_x, *rest,
+    slot_ref, order_ref, q_ref, k_ref, v_ref, dctx_ref, ctxt_ref, lse_ref, base_ref, step_ref, p_ref, go_ref, xn_ref, gm_ref,
+    out_ref, sum_ref, go_in, gq_ref, gm_out,
+    qm, dom, do_slots, do_sorted, kt, delta, dqt, dk_buf, dv_buf, d_blocks, acc, x_buf, gm_in, gm_sum,
+    l_x, l_m, s_x, r_x, *rest,
 ):
     bufs, sems = rest[:4], rest[4:]
-    sc = Scatter(lambda zs, part: p_ref.at[zs, :, 1 - sc.c, part, :], bufs, sems[3:], nz)
+    sc = Scatter(lambda zs, part: p_ref.at[zs, :, 1 - sc.c, part, :], bufs, sems[9:], nz)
+    n_early = early_blocks(nz * 4)
+    mlp = MlpBlocks(gm_ref, gm_in, gm_sum, gm_out, sems[3:9], nz, n_dp, 1, n_early)
     moves = Exchange(
         lambda t: dctx_ref.at[:, pl.ds(pl.multiple_of(t * 2 * HEAD_DIM, 128), 2 * HEAD_DIM)],
         lambda t: do_slots.at[t],
@@ -723,16 +819,20 @@
 
     d = lax.axis_index("dp")
 
-    def x_copy(r):
+    def x_copy(i, r):
         t = (d + r) % n_dp
-        return remote(go_ref.at[t], go_in.at[r], s_x.at[r], r_x.at[r], dp=t)
-
+        zs = outermost(i, nz)
+        return remote(go_ref.at[t, zs], go_in.at[r, zs], s_x.at[i, r], r_x.at[i, r], dp=t)
+
+    mlp.load()
     greet_all(nz, n_dp)
     moves.start()
+    mlp.start()
 
     @pl.loop(1, n_dp)
     def _(r):
-        x_copy(r).start()
+        for i in range(nz - 1):
+            x_copy(i, r).start()
 
     @pl.loop(0, sc.units)
     def _(k):
@@ -744,6 +844,9 @@
         load(k).wait()
         sc.chip_sum(k)
 
+    for e in range(2):
+        sc.later(1 + e, sum_ref)
+        mlp.add(1 + e)
     moves.arrive()
     length = q_ref.shape[0]
     width = 2 * HEAD_DIM
@@ -779,7 +882,12 @@
 
     @pl.loop(0, n_tiles)
     def _(j):
-        sc.later(j + 1, sum_ref)
+        sc.later(j + 3, sum_ref)
+
+        @pl.when(j + 3 < mlp.last)
+        def _():
+            mlp.add(j + 3)
+
         rows_k = pl.ds(pl.multiple_of(j * tile, tile), tile)
         keys = k_ref[rows_k, :]
         vals = v_ref[rows_k, :]
@@ -832,50 +940,54 @@
     x_load(0).start()
     acc[...] = jnp.zeros_like(acc)
 
-    @pl.loop(n_tiles + 1, sc.steps)
-    def _(k):
-        for j in range(2):
-            p = 2 * (k - n_tiles - 1) + j
-
-            @pl.when(p < pairs)
+    first = n_tiles + 3
+
+    @pl.loop(0, max(sc.steps - first, pairs))
+    def _(p):
+        @pl.when(p < pairs)
+        def _():
+            @pl.when(p + 1 < pairs)
             def _():
-                @pl.when(p + 1 < pairs)
-                def _():
-                    x_load(p + 1).start()
-
-                x_load(p).wait()
-                d_pair = out_ref[pl.ds(2 * p, 2)].reshape(2 * block, 3 * width)
-                acc[...] += dot_tn(x_buf[p % 2], d_pair)
-
-        sc.later(k, sum_ref)
+                x_load(p + 1).start()
+
+            x_load(p).wait()
+            d_pair = out_ref[pl.ds(2 * p, 2)].reshape(2 * block, 3 * width)
+            acc[...] += dot_tn(x_buf[p % 2], d_pair)
+
+        @pl.when(first + p < sc.steps)
+        def _():
+            sc.later(first + p, sum_ref)
 
     gq_ref[...] = acc[...].astype(BF16)
     moves.drain()
     sc.drain()
+    mlp.finish()
 
     @pl.loop(1, n_dp)
     def _(r):
-        x_copy(r).wait()
+        for i in range(nz - 1):
+            x_copy(i, r).wait()
 
 
 def attn_bwd(
-    slot_of_block, order, q, k, v, d_ctx, ctxt, lse, base, step, partial, grad_out, xn, nz, tile
+    slot_of_block, order, q, k, v, d_ctx, ctxt, lse, base, step, partial, grad_out, xn, grad_mlp, nz, tile
 ):
     length, width = q.shape
     block, wide = d_ctx.shape
     whole = pl.BlockSpec(memory_space=pltpu.VMEM)
     smem = pl.BlockSpec(memory_space=pltpu.SMEM)
     any_spec = pl.BlockSpec(memory_space=pl.ANY)
-    n_dp = grad_out.shape[0]
-    d_qkv, summed, grad_out_in, grad_qkv = pl.pallas_call(
+    n_dp, peers, shard, cols_mlp = grad_mlp.shape
+    d_qkv, summed, grad_out_in, grad_qkv, grad_mlp = pl.pallas_call(
         functools.partial(attn_bwd_kernel, nz, n_dp, block, tile),
-        in_specs=[smem, smem] + [whole] * 3 + [any_spec] + [whole] * 4 + [any_spec] * 3,
-        out_specs=[whole, whole, any_spec, whole],
+        in_specs=[smem, smem] + [whole] * 3 + [any_spec] + [whole] * 4 + [any_spec] * 4,
+        out_specs=[whole, whole, any_spec, whole, any_spec],
         out_shape=[
             jax.ShapeDtypeStruct((length // block, block, 3 * width), BF16),
             jax.ShapeDtypeStruct((block, wide), F32),
             jax.ShapeDtypeStruct(grad_out.shape, BF16),
             jax.ShapeDtypeStruct((wide, 3 * width), BF16),
+            jax.ShapeDtypeStruct((peers, shard, cols_mlp), BF16),
         ],
         scratch_shapes=[
             pltpu.VMEM((2, length, width), BF16),
@@ -890,13 +1002,16 @@
             pltpu.VMEM((length // block, block, 3 * width), BF16),
             pltpu.VMEM((wide, 3 * width), F32),
             pltpu.VMEM((2, 2 * block, wide), BF16),
+            pltpu.VMEM((n_dp - 1, early_blocks(peers), shard, cols_mlp), BF16),
+            pltpu.VMEM((early_blocks(peers), shard, cols_mlp), BF16),
             pltpu.SemaphoreType.DMA((2,)),
             pltpu.SemaphoreType.DMA((nz * CHUNKS,)),
-            pltpu.SemaphoreType.DMA((n_dp,)),
-            pltpu.SemaphoreType.DMA((n_dp,)),
+            pltpu.SemaphoreType.DMA((nz - 1, n_dp)),
+            pltpu.SemaphoreType.DMA((nz - 1, n_dp)),
         ]
         + scatter_buffers(nz, block, wide)
         + exchange_sems(nz)
+        + mlp_block_sems(nz, n_dp, early_blocks(peers))
         + scatter_sems(nz),
         compiler_params=pltpu.CompilerParams(
             vmem_limit_bytes=VMEM_LIMIT, collective_id=6, has_side_effects=True
@@ -909,9 +1024,10 @@
         name="attn_bwd",
     )(
         slot_of_block, order, q, k, v, d_ctx, ctxt, lse, base, step,
-        partial.reshape(nz, 2, 2, block, wide), grad_out, xn.reshape(2 * nz, 2 * block, wide),
-    )
-    return d_qkv.reshape(length, 3 * width), summed, grad_out_in, grad_qkv
+        partial.reshape(nz, 2, 2, block, wide), grad_out,
+        xn.reshape(2 * nz, 2 * block, wide), grad_mlp,
+    )
+    return d_qkv.reshape(length, 3 * width), summed, grad_out_in, grad_qkv, grad_mlp
 
 
 def scatter_mlp_kernel(
@@ -945,6 +1061,7 @@
             )
         ]
 
+    every = sc.units // pairs
     greet_neighbours(nz)
 
     @pl.loop(0, sc.units)
@@ -972,17 +1089,24 @@
             acc[at, 0:gate_up] += dot_tn(x_buf[s, :, at], dgu_buf[s])
             acc[at, gate_up:] += dot_tn(c_buf[s, :, at], hid_buf[s])
 
+    def chip_sum(k):
+        load(k).wait()
+        sc.chip_sum(k)
+
+    for k in range(2):
+        chip_sum(k)
+
     @pl.loop(0, sc.steps)
     def _(k):
-        @pl.when(k < sc.units)
-        def _():
-            load(k).wait()
-
-        sc.step(k, out_ref)
-
-        @pl.when(k < pairs)
-        def _():
-            weight_grads(k)
+        @pl.when(k + 2 < sc.units)
+        def _():
+            chip_sum(k + 2)
+
+        sc.later(k, out_ref)
+
+        @pl.when(jnp.logical_and(k % every == 0, k // every < pairs))
+        def _():
+            weight_grads(k // every)
 
     grad_ref[...] = acc[...].astype(BF16)
     sc.drain()
@@ -1045,105 +1169,109 @@
 def scatter_last_kernel(
     nz, n_dp, dq_ref, w_ref, gq_ref, gm_ref, go_ref, go_in,
     out_ref, gq_out, gm_out,
-    theirs, gq_in, gq_sum, gm_in, gm_sum, go_buf,
-    l_o, l_q, s_xq, r_xq, own_q, s_q, r_q, l_m, s_xm, r_xm, own_m, s_m, r_m, *rest,
+    theirs, gq_in, gq_sum, gm_in, gm_sum, go_buf, go_early,
+    l_o, s_xo, r_xo, l_q, s_xq, r_xq, *rest,
 ):
     bufs, sems = rest[:4], rest[4:]
-    sc = Scatter(lambda zs, part: theirs.at[zs, :, part, :], bufs, sems, nz)
+    sc = Scatter(lambda zs, part: theirs.at[zs, :, part, :], bufs, sems[9:], nz, FINE)
     mine = bufs[0]
     d = lax.axis_index("dp")
     rows, width = dq_ref.shape[3], mine.shape[3]
     shard = gq_in.shape[2]
     cols = dq_ref.shape[4]
-    gq_moves = Exchange(
-        lambda t: gq_sum.at[t], lambda t: gq_out.at[t], (s_q, r_q, own_q), nz
-    )
-    gm_moves = Exchange(
-        lambda t: gm_sum.at[t], lambda t: gm_out.at[t], (s_m, r_m, own_m), nz
-    )
-
+    gq_moves = Exchange(lambda t: gq_sum.at[t], lambda t: gq_out.at[t], sems[:3], nz)
+    n_early = early_blocks(nz * 4)
+    mlp = MlpBlocks(
+        gm_ref, gm_in, gm_sum, gm_out, sems[3:9], nz, n_dp, 1 + n_early, nz * 4 - n_early
+    )
     keep_q = pltpu.make_async_copy(gq_ref.at[d], gq_in.at[0], l_q)
     keep_q.start()
-    keep_m = pltpu.make_async_copy(gm_ref.at[d], gm_sum, l_m)
-    keep_m.start()
+    mlp.load()
 
     def xq_copy(r):
         t = (d + r) % n_dp
         return remote(gq_ref.at[t], gq_in.at[r], s_xq.at[r], r_xq.at[r], dp=t)
 
-    def xm_copy(i, r):
-        t = (gm_moves.me + i) % gm_moves.peers
-        dp = (d + r) % n_dp
-        return remote(gm_ref.at[dp, t], gm_in.at[r - 1, t], s_xm.at[i, r], r_xm.at[i, r], dp=dp)
+    def xo_copy(r):
+        t = (d + r) % n_dp
+        zs = outermost(nz - 1, nz)
+        return remote(go_ref.at[t, zs], go_buf.at[r], s_xo.at[r], r_xo.at[r], dp=t)
 
     greet_all(nz, n_dp)
 
     @pl.loop(1, n_dp)
     def _(r):
         xq_copy(r).start()
-
-        @pl.loop(1, gm_moves.peers + 1)
-        def _(i):
-            xm_copy(i, r).start()
+        xo_copy(r).start()
+
+    mlp.start()
 
     def partial_sums(zs, core):
         left = dq_ref[zs, :, core].reshape(2 * rows, cols)
         return dot_nt(left, w_ref[:, 0:cols]).astype(BF16).reshape(2, rows, width)
 
-    def out_loads(zs):
-        own = pltpu.make_async_copy(go_ref.at[d, zs], go_buf.at[0], l_o.at[0])
+    def out_loads(zs, last):
+        own = pltpu.make_async_copy(go_ref.at[d, zs], buf_of(last).at[0], l_o.at[0])
         return [own] + [
-            pltpu.make_async_copy(go_in.at[r, zs], go_buf.at[r], l_o.at[r]) for r in range(1, n_dp)
+            xo_copy(r)
+            if last
+            else pltpu.make_async_copy(go_in.at[r, zs], go_early.at[r], l_o.at[r])
+            for r in range(1, n_dp)
         ]
 
-    def out_sums(core):
-        return sum(go_buf[r, :, core].astype(F32) for r in range(n_dp)).astype(BF16)
+    def buf_of(last):
+        return go_buf if last else go_early
+
+    def out_sums(core, last):
+        return sum(buf_of(last)[r, :, core].astype(F32) for r in range(n_dp)).astype(BF16)
 
     if mine.shape[2] > rows + shard:
         for buf in (mine, theirs):
             buf[:, :, rows + shard :, :] = jnp.zeros_like(buf[:, :, rows + shard :, :])
 
-    def produce(i):
-        zs = jnp.where(i % 2 == 0, nz - 1 - i // 2, i // 2)
-        for copy in out_loads(zs):
-            copy.start()
+    def produce(i, last):
+        zs = outermost(i, nz)
+        loads = out_loads(zs, last)
+        loads[0].start()
+        if not last:
+            for copy in loads[1:]:
+                copy.start()
         theirs[zs, :, 0:rows, :] = partial_sums(zs, 1 - sc.c)
-        for copy in out_loads(zs):
-            copy.wait()
-        theirs[zs, :, rows : rows + shard, :] = out_sums(1 - sc.c)
-        for q in range(CHUNKS):
-            sc.to_sibling(2 * CHUNKS * (i // 2) + 2 * q + i % 2).start()
+        loads[0].wait()
+        for copy in loads[1:]:
+            if last:
+                copy.wait_recv()
+            else:
+                copy.wait()
+        theirs[zs, :, rows : rows + shard, :] = out_sums(1 - sc.c, last)
+        for q in range(FINE):
+            sc.to_sibling(2 * FINE * (i // 2) + 2 * q + i % 2).start()
         mine[zs, :, 0:rows, :] = partial_sums(zs, sc.c)
-        mine[zs, :, rows : rows + shard, :] = out_sums(sc.c)
+        mine[zs, :, rows : rows + shard, :] = out_sums(sc.c, last)
 
     @pl.loop(0, 2)
     def _(i):
-        produce(i)
-
-    keep_m.wait()
-
-    def mlp_block(i):
-        t = (gm_moves.me + i) % gm_moves.peers
-        @pl.loop(1, n_dp)
-        def _(r):
-            xm_copy(i, r).wait_recv()
-            gm_sum[t] = (gm_sum[t].astype(F32) + gm_in[r - 1, t].astype(F32)).astype(BF16)
-
-        @pl.when(i < gm_moves.peers)
-        def _():
-            gm_moves.copy(i).start()
-
-        @pl.when(i == gm_moves.peers)
-        def _():
-            gm_moves.keep().start()
+        produce(i, False)
+
+    @pl.loop(0, 2)
+    def _(i):
+        sc.chip_sum(i)
 
     @pl.loop(0, sc.steps)
     def _(k):
-        sc.step(k, out_ref)
-
-        @pl.when(k < nz - 2)
-        def _():
-            produce(k + 2)
+        @pl.when(k + 2 < sc.units)
+        def _():
+            sc.chip_sum(k + 2)
+
+        sc.later(k, out_ref)
+
+        @pl.when(jnp.logical_and(k >= 1, k < nz - 2))
+        def _():
+            produce(k + 1, False)
+
+        @pl.when(k == nz + 1)
+        def _():
+            produce(nz - 1, True)
 
         @pl.when(k == 1)
         def _():
@@ -1157,25 +1285,21 @@
 
             gq_moves.start()
 
-        for j in range(2):
-            i = 2 * (k - 2) + 1 + j
-
-            @pl.when(jnp.logical_and(i >= 1, i <= gm_moves.peers))
-            def _():
-                mlp_block(i)
+        i = mlp.first + k - 7
+
+        @pl.when(jnp.logical_and(i >= mlp.first, i < mlp.last))
+        def _():
+            mlp.add(i)
 
     sc.drain()
-    for moves in (gq_moves, gm_moves):
-        moves.arrive()
-        moves.drain()
+    gq_moves.arrive()
+    gq_moves.drain()
+    mlp.finish()
 
     @pl.loop(1, n_dp)
     def _(r):
         xq_copy(r).wait_send()
-
-        @pl.loop(1, gm_moves.peers + 1)
-        def _(i):
-            xm_copy(i, r).wait_send()
+        xo_copy(r).wait_send()
 
 
 def scatter_last(d_qkv, w, grad_qkv, grad_mlp, grad_out, grad_out_in, nz, n_dp, collective_id):
@@ -1183,8 +1307,8 @@
     rows, cols = d_qkv.shape[0] // peers, d_qkv.shape[1]
     width = w.shape[0]
     shard = width // (n_dp * peers)
-    cols_mlp = grad_mlp.shape[1]
-    all_rows = rows + max(shard, 16 * CHUNKS)
+    cols_mlp = grad_mlp.shape[3]
+    all_rows = rows + max(shard, 16 * FINE)
     any_spec = pl.BlockSpec(memory_space=pl.ANY)
     vmem = pl.BlockSpec(memory_space=pltpu.VMEM)
     dma = pltpu.SemaphoreType.DMA
@@ -1201,25 +1325,21 @@
             pltpu.VMEM((nz, 2, all_rows, width), BF16),
             pltpu.VMEM((n_dp, peers, shard, cols), BF16),
             pltpu.VMEM((peers, shard, cols), BF16),
-            pltpu.VMEM((n_dp - 1, peers, shard, cols_mlp), BF16),
-            pltpu.VMEM((peers, shard, cols_mlp), BF16),
+            pltpu.VMEM((n_dp - 1, peers - early_blocks(peers), shard, cols_mlp), BF16),
+            pltpu.VMEM((peers - early_blocks(peers), shard, cols_mlp), BF16),
             pltpu.VMEM((n_dp, 2, 2, shard, width), BF16),
+            pltpu.VMEM((n_dp, 2, 2, shard, width), BF16),
+            dma((n_dp,)),
+            dma((n_dp,)),
             dma((n_dp,)),
             dma,
             dma((n_dp,)),
             dma((n_dp,)),
-            dma,
-            dma((peers,)),
-            dma((peers,)),
-            dma,
-            dma((peers + 1, n_dp)),
-            dma((peers + 1, n_dp)),
-            dma,
-            dma((peers,)),
-            dma((peers,)),
         ]
         + scatter_buffers(nz, all_rows, width)
-        + scatter_sems(nz),
+        + exchange_sems(nz)
+        + mlp_block_sems(nz, n_dp, peers - early_blocks(peers))
+        + scatter_sems(nz, FINE),
         compiler_params=pltpu.CompilerParams(
             vmem_limit_bytes=VMEM_LIMIT, collective_id=collective_id, has_side_effects=True
         ),
@@ -1233,18 +1353,30 @@
         d_qkv.reshape(nz, 2, 2, rows, cols),
         w,
         grad_qkv.reshape(n_dp, peers, shard, cols),
-        grad_mlp.reshape(n_dp, peers, shard, cols_mlp),
+        grad_mlp,
         grad_out.reshape(n_dp, nz, 2, 2, shard, width),
         grad_out_in.reshape(n_dp, nz, 2, 2, shard, width),
     )
 
 
 def layout_kernel(
-    gq_ref, gm_ref, wq_ref, wgu_ref, g1_ref, g2_ref, q_out, gu_out, down_out, g1_out, g2_out
+    gq_ref, gm_early, gm_late, wq_ref, wgu_ref, g1_ref, g2_ref, sum_ref, x_ref, gain_ref, dmid_ref, y_ref, mlp_ref,
+    q_out, gu_out, down_out, g1_out, g2_out, layer_out, tok_out, wout_out,
 ):
+    rows = x_ref.shape[0]
+    layer_out[...] = (y_ref[...] + mlp_ref[...]).astype(BF16)
+    wout_out[...] = sum_ref[rows : rows + wout_out.shape[0], :]
+    x = x_ref[...].astype(F32)
+    scaled = sum_ref[0:rows, :] * gain_ref[0:1, :]
+    inverse = lax.rsqrt(jnp.mean(x * x, axis=1, keepdims=True) + EPS)
+    along = jnp.mean(scaled * x, axis=1, keepdims=True) * (inverse * inverse)
+    tok_out[...] = dmid_ref[...] + inverse * (scaled - x * along)
+
     peers = gq_ref.shape[0]
     part_q = gq_ref.shape[2] // 3
-    hid = gm_ref.shape[2] // 3
+    hid = gm_early.shape[2] // 3
+    z, y, c = position()
+    me = z * 4 + y * 2 + c
     sum_q = jnp.zeros((gq_ref.shape[1], part_q), F32)
     sum_m = jnp.zeros((gq_ref.shape[1], hid), F32)
     for t in range(peers):
@@ -1253,34 +1385,49 @@
             block = gq_ref[t, :, s * part_q : (s + 1) * part_q].astype(F32)
             q_out[:, at] = block
             sum_q += block * wq_ref[:, at].astype(F32)
+        far = (me - t + peers - 1) % peers + 1
+        from_t = jnp.where(far <= early_blocks(peers), gm_early[t], gm_late[t]).astype(F32)
         for s in range(2):
             at = pl.ds((s * peers + t) * hid, hid)
-            block = gm_ref[t, :, s * hid : (s + 1) * hid].astype(F32)
+            block = from_t[:, s * hid : (s + 1) * hid]
             gu_out[:, at] = block
             sum_m += block * wgu_ref[:, at].astype(F32)
-        down_out[:, t * hid : (t + 1) * hid] = gm_ref[t, :, 2 * hid :].astype(F32)
-    g1_out[...] = jnp.sum(sum_q, axis=1, keepdims=True) / g1_ref[...].astype(F32)
-    g2_out[...] = jnp.sum(sum_m, axis=1, keepdims=True) / g2_ref[...].astype(F32)
-
-
-def layout_call(grad_qkv, grad_mlp, w_qkv, w_gate_up, gain_one, gain_two):
+        down_out[:, t * hid : (t + 1) * hid] = from_t[:, 2 * hid :]
+
+    def as_row(sums):
+        column = jnp.sum(sums, axis=1, keepdims=True)
+        return jnp.broadcast_to(column, (column.shape[0], 128)).T[0:1, :]
+
+    g1_out[...] = as_row(sum_q) / g1_ref[...].astype(F32)
+    g2_out[...] = as_row(sum_m) / g2_ref[...].astype(F32)
+
+
+def layout_call(
+    grad_qkv, mlp_early, mlp_late, w_qkv, w_gate_up, gain_one, gain_two, sums, tokens, gains, d_mid, y_mid, mlp_out
+):
     shard = w_qkv.shape[0]
     hidden = w_gate_up.shape[1] // 2
     vmem = pl.BlockSpec(memory_space=pltpu.VMEM)
     return pl.pallas_call(
         layout_kernel,
-        in_specs=[vmem] * 6,
-        out_specs=[vmem] * 5,
+        in_specs=[vmem] * 13,
+        out_specs=[vmem] * 8,
         out_shape=[
             jax.ShapeDtypeStruct(w_qkv.shape, F32),
             jax.ShapeDtypeStruct(w_gate_up.shape, F32),
             jax.ShapeDtypeStruct((shard, hidden), F32),
-            jax.ShapeDtypeStruct((shard, 1), F32),
-            jax.ShapeDtypeStruct((shard, 1), F32),
+            jax.ShapeDtypeStruct((1, shard), F32),
+            jax.ShapeDtypeStruct((1, shard), F32),
+            jax.ShapeDtypeStruct(tokens.shape, BF16),
+            jax.ShapeDtypeStruct(tokens.shape, F32),
+            jax.ShapeDtypeStruct((shard, tokens.shape[1]), F32),
         ],
         compiler_params=pltpu.CompilerParams(vmem_limit_bytes=VMEM_LIMIT),
         name="layout",
-    )(grad_qkv, grad_mlp, w_qkv, w_gate_up, gain_one[:, None], gain_two[:, None])
+    )(
+        grad_qkv, mlp_early, mlp_late, w_qkv, w_gate_up, gain_one[None], gain_two[None],
+        sums, tokens, gains, d_mid, y_mid, mlp_out,
+    )
 
 
 def gather_qkv_kernel(
@@ -1730,7 +1877,7 @@
     )
 
     x_float = tokens.astype(F32)
-    gain_one, gain_two = gains[0], gains[1]
+    gain_two = gains[1]
     y_mid = x_float + dot_nn(ctx_tok, wout_full)
     xn2 = rms_scale(y_mid, gain_two).astype(BF16)
 
@@ -1744,24 +1891,22 @@
     d_mid_b = d_mid.astype(BF16)
 
     d_ctx = dot_nt(d_mid_b, wout_full).astype(BF16)
-    grad_out = dot_tn(ctx_tok, d_mid_b).astype(BF16).reshape(n_dp, groups * shard, width)
-
-    d_qkv, mlp_out, grad_out_in, grad_qkv = attn_bwd(
+    grad_out = dot_tn(ctx_tok, d_mid_b).astype(BF16).reshape(n_dp, nz, 2, 2, shard, width)
+    grad_mlp = grad_mlp.reshape(n_dp, groups, shard, -1)
+
+    d_qkv, mlp_out, grad_out_in, grad_qkv, mlp_early = attn_bwd(
         slot_of_block, order, q, k, v, d_ctx, ctxt, lse, base, step, out_part, grad_out, xn1_all,
-        nz, 512,
-    )
-    layer_out = (y_mid + mlp_out).astype(BF16)
-    sums, grad_qkv, grad_mlp = scatter_last(
+        grad_mlp, nz, 512,
+    )
+    sums, grad_qkv, mlp_late = scatter_last(
         d_qkv, wqkv_mine, grad_qkv, grad_mlp, grad_out, grad_out_in, nz, n_dp, 4
     )
-    d_xn1, out_rows = sums[:tok_rows], sums[tok_rows : tok_rows + shard]
-    qkv_rows, gu_rows, down_rows, grad_gain_one, grad_gain_two = layout_call(
-        grad_qkv, grad_mlp, w_qkv, w_gate_up, gain_attn, gain_mlp
-    )
-
-    _, pull_one = jax.vjp(lambda v: rms_scale(v, gain_one), x_float)
-    (dx_norm,) = pull_one(d_xn1)
-    grad_tokens = d_mid + dx_norm
+    (
+        qkv_rows, gu_rows, down_rows, grad_gain_one, grad_gain_two, layer_out, grad_tokens, out_rows,
+    ) = layout_call(
+        grad_qkv, mlp_early, mlp_late, w_qkv, w_gate_up, gain_attn, gain_mlp,
+        sums, tokens, gains, d_mid, y_mid, mlp_out,
+    )
     return (
         layer_out,
         grad_tokens,

time: 801 us -> 802 us (level)
    pallas_call x1, Pallas kernels: 188 us -> 176 us  [scatter_last(): pl.pallas_call(functools.partial(scatter_last_kernel, nz, n_dp), in_specs...]
    pallas_call x1, Pallas kernels: 113 us -> 121 us  [attn_bwd(): pl.pallas_call(functools.partial(attn_bwd_kernel, nz, n_dp, block, tile),...]
where the time goes in v2:
time: 802 us; the launch traced here: 795 us
  Pallas kernels  762 us (95%)
  matrix products  18.9 us (2%)
  other arithmetic  10.7 us (1%)
    pallas_call x1, Pallas kernels, scatter_last(): pl.pallas_call(functools.partial(scatter_last_kernel, nz, n_dp), in_specs...  176 us
    pallas_call x1, Pallas kernels, gather_qkv(): pl.pallas_call(functools.partial(gather_qkv_kernel, nz, n_dp), in_specs=[...  166 us
    pallas_call x1, Pallas kernels, attn_bwd(): pl.pallas_call(functools.partial(attn_bwd_kernel, nz, n_dp, block, tile),...  121 us
    pallas_call x1, Pallas kernels, scatter_mlp(): pl.pallas_call(functools.partial(scatter_mlp_kernel, nz), in_specs=[any_s...  108 us
    pallas_call x1, Pallas kernels, attn_fwd(): pl.pallas_call(functools.partial(attn_fwd_kernel, nz, n_dp, block, tile),...  99.7 us
    pallas_call x1, Pallas kernels, gather_mlp(): pl.pallas_call(functools.partial(gather_mlp_kernel, nz, n_dp), in_specs=[...  79.9 us

profile of v2, /device:TPU:13, one launch (start us, length us, event | category | flops | bytes accessed | tf_op | source)
XLA Modules:
  0.0 795.2 jit_solution(6778222537225036759)
XLA Ops:
  0.6 0.0 copy-start.3
  0.6 0.8 pad_maximum_fusion.3
  1.4 1.9 sort.17
  3.3 0.1 copy.23
  3.4 0.8 multiply_cosine_fusion.1
  4.2 0.6 pad_maximum_fusion.2.base_ref
  4.9 1.1 broadcast_multiply_fusion.1
  6.0 0.8 pad_maximum_fusion.1.step_ref
  6.8 0.0 copy-done.3
  6.8 0.1 copy.24
  6.9 0.5 copy.26
  7.4 0.7 reshape.369
  8.1 1.1 pad_maximum_fusion.wq_ref
  9.2 165.9 %gather_qkv.1 = (bf16[8,384,2048]{2,1,0:T(8,128)(2,1)}, f32[8,384,384]{2,1,0:T(8,128)}, f32[8,2048]{1,0:T(8,128)}, bf16[2048,512]{1,0:T(8,128)(2,1)}, bf16[1024,...) custom-call(bf16[192,2048]{1,0:T(8,128)(2,1)} %x_ref.1, bf16[16,64,512]{2,1,0:T(8,128)(2,1)} %pad_maximum_fusion.wq_ref, ...), custom_call_target="tpu_custom_call" | custom-call | flops 4831838208 | bytes 377487360 | tf_op jit(solution)/shard_map/gather_qkv/pallas_call | solution.py:1620
  175.1 0.8 slice.3
  176.0 99.7 %attn_fwd.1 = (bf16[3072,128]{1,0:T(8,128)(2,1)}, bf16[3072,128]{1,0:T(8,128)(2,1)}, bf16[3072,128]{1,0:T(8,128)(2,1)}, f32[128,3072]{1,0:T(8,128)}, f32[2,3072]...) custom-call(s32[16]{0:T(128)} %get-tuple-element.46.slot_ref, ...), custom_call_target="tpu_custom_call" | custom-call | flops 12079595520 | bytes 188743680 | tf_op jit(solution)/shard_map/attn_fwd/pallas_call | solution.py:755
  275.7 0.0 copy-done.5
  275.7 5.6 multiply_reduce_fusion.1
  281.3 1.3 multiply_convert_fusion.x_ref
  282.6 79.9 %gather_mlp.1 = (bf16[4,2,2,192,2048]{4,3,2,1,0:T(8,128)(2,1)}, bf16[8,384,2048]{2,1,0:T(8,128)(2,1)}, bf16[8,384,2048]{2,1,0:T(8,128)(2,1)}, bf16[8,384,512]{2,1,0:T(8,128)(2,1)}, bf16[8,384,1024]{2,1,0:T(8,128)(2,1)}) custom-call(bf16[192,2048]{1,0:T(8,128)(2,1)} %multiply_convert_fusion.x_ref, bf16[8,384,2048]{2,1,0:T(8,128)(2,1)} %bitcast.50, ...), custom_call_target="tpu_custom_call" | custom-call | flops 38654705664 | bytes 377487360 | tf_op jit(solution)/shard_map/gather_mlp/pallas_call | solution.py:1796
  362.5 107.5 %scatter_mlp.1 = (f32[192,2048]{1,0:T(8,128)}, bf16[2048,1536]{1,0:T(8,128)(2,1)}) custom-call(bf16[4,2,2,192,2048]{4,3,2,1,0:T(8,128)(2,1)} %bitcast.53, bf16[8,384,2048]{2,1,0:T(8,128)(2,1)} %bitcast.52, bf16[8,384,2048]{2,1,0:T(8,128)(2,1)} %bitcast.51, bf16[8,384,1024]{2,1,0:T(8,128)(2,1)} %get-tuple-element.59.dgu_ref, ...), custom_call_target="tpu_custom_call" | custom-call | flops 19327352832 | bytes 377487360 | tf_op jit(solution)/shard_map/scatter_mlp/pallas_call | solution.py:1129
  470.1 0.0 copy-start.6
  470.1 1.9 multiply_reduce_fusion
  472.0 0.2 copy-done.6
  472.1 0.5 fusion.dmid_ref
  472.6 0.0 copy-start.1
  472.6 0.0 copy-start.4
  472.6 7.8 convolution_convert_fusion.1.dctx_ref
  480.4 5.6 convolution_convert_fusion
  486.0 121.1 %attn_bwd.1 = (bf16[16,192,384]{2,1,0:T(8,128)(2,1)}, f32[192,2048]{1,0:T(8,128)}, bf16[2,4,2,2,64,2048]{5,4,3,2,1,0:T(8,128)(2,1)}, bf16[2048,384]{1,0:T(8,128)(2,1)}, bf16[16,64,1536]{2,1,0:T(8,128)(2,1)}) custom-call(s32[16]{0:T(128)} %get-tuple-element.46.slot_ref, s32[16]{0:T(128)} %bitcast.46, bf16[3072,128]{1,0:T(8,128)(2,1)} %get-tuple-element.49.q_ref, ...), custom_call_target="tpu_custom_call" | custom-call | flops 30198988800 | bytes 377487360 | tf_op jit(solution)/shard_map/attn_bwd/pallas_call | solution.py:981
  607.1 175.7 %scatter_last.1 = (f32[256,2048]{1,0:T(8,128)}, bf16[16,64,384]{2,1,0:T(8,128)(2,1)}, bf16[16,64,1536]{2,1,0:T(8,128)(2,1)}) custom-call(bf16[4,2,2,192,384]{4,3,2,1,0:T(8,128)(2,1)} %bitcast.35, bf16[2048,512]{1,0:T(8,128)(2,1)} %get-tuple-element.68.w_ref, bf16[2,16,64,384]{3,2,1,0:T(8,128)(2,1)} %bitcast.36, bf16[2,16,64,1536]{3,2,1,0:T(8,128)(2,1)} %bitcast.31, ...), custom_call_target="tpu_custom_call" | custom-call | flops 4831838208 | bytes 377487360 | tf_op jit(solution)/shard_map/scatter_last/pallas_call | solution.py:1315
  782.8 12.0 %layout.1 = (f32[64,6144]{1,0:T(8,128)}, f32[64,16384]{1,0:T(8,128)}, f32[64,8192]{1,0:T(8,128)}, f32[1,64]{1,0:T(1,128)}, f32[1,64]{1,0:T(1,128)}, /*index=5*/b...) custom-call(bf16[16,64,384]{2,1,0:T(8,128)(2,1)} %get-tuple-element.71.gq_ref, ...), custom_call_target="tpu_custom_call" | custom-call | tf_op jit(solution)/shard_map/layout/pallas_call | solution.py:1411
  (14 shorter events, 0.1 us)
Async XLA Ops:
  0.6 6.1 copy-start.3
  176.0 99.7 %copy-start.5 = (bf16[192,2048]{1,0:T(8,128)(2,1)S(1)}, bf16[192,2048]{1,0:T(8,128)(2,1)}, u32[]{:S(2)}) copy-start(bf16[192,2048]{1,0:T(8,128)(2,1)} %x_ref.1) | copy-start | bytes 2359300
  281.3 190.7 %copy-start = (f32[192,2048]{1,0:T(8,128)}, f32[192,2048]{1,0:T(8,128)S(1)}, u32[]{:S(2)}) copy-start(f32[192,2048]{1,0:T(8,128)S(1)} %get-tuple-element.91.y_ref) | copy-start | bytes 4718596
  470.0 1.9 copy-start.2
  470.1 2.1 copy-start.6
  472.6 7.8 copy-start.1
  472.6 7.8 copy-start.4
